TPU v7x, 512 devices: a whole 4x8x8 slice. The times are simulated.
512 devices in a mesh: query: 16 (over z, core), passage: 32 (over y, x).
Axes of the slice: x: 4, y: 8, z: 8, core: 2. Of those that a mesh axis runs over, the one named last changes fastest.
Arguments:
- query_tokens: bfloat16 [512, 32, 128], P(('query', 'passage')), may hold values from -3 to 3
- passage_tokens: bfloat16 [2048, 128, 128], P('passage'), may hold values from -3 to 3
- passage_lengths: int32 [2048], replicated, may hold values from 32 to 128
- cand_shard: int32 [512, 256, 1], P('query'), may hold values from 0 to 31; in each aligned block of 8192 rows (0 to 8191, 8192 to 16383, ..., all dimensions but the last counted through in order) at most 512 rows name the same one
- cand_local: int32 [512, 256], P('query'), may hold values from 0 to 63
- teacher_scores: float32 [512, 256], P('query'), may hold values from -20 to 320
Outputs:
- loss: float32 [], replicated
- query_grads: float32 [512, 32, 128], P(('query', 'passage'))
Inputs may be any that keep to these rules, and one draw needn't show every extreme that they name: `cand_shard`: within one group's list (aligned blocks of 8192 entries), no shard is named more than 512 times; in some group some shard is named exactly 512 times.
All inputs are finite; a program needn't handle non-finite values.
Results may differ from a plain program's by a relative error of at most 0.003.
Values may be sent and summed in bfloat16 or wider, within the bound.
No kernel may reach another device: no remote copies, remote signals or barrier semaphores. Data moves between devices by JAX's collectives and lax.ppermute only.
A program may use at most 64 MiB of HBM per device.

v0:
```python
import jax
import jax.numpy as jnp
from jax import lax
from jax.sharding import PartitionSpec as P

CAND = 256
BLOCK = 128
MOST = 512


sharpness = 2.0
floor_logit = -1e30


def token_softmax(query_rows, passage_rows, lengths):
    sims = jnp.einsum("bid,bjd->bij", query_rows, passage_rows, preferred_element_type=jnp.float32)
    in_length = jnp.arange(passage_rows.shape[1])[None, None, :] < lengths[:, None, None]
    logits = jnp.where(in_length, sharpness * sims, floor_logit)
    row_top = jnp.max(logits, axis=2, keepdims=True)
    exp_terms = jnp.where(in_length, jnp.exp(logits - row_top), 0.0)
    sum_exp = jnp.sum(exp_terms, axis=2, keepdims=True)
    scores = jnp.sum(row_top[..., 0] + jnp.log(sum_exp[..., 0]), axis=1) / sharpness
    weights = (exp_terms / sum_exp).astype(jnp.bfloat16)
    return (scores, weights)


def shard_slots(shard_flat, target, capacity):
    entry_count = shard_flat.shape[0]
    positions = jnp.arange(entry_count, dtype=jnp.int32)
    on_target = shard_flat == target
    sort_keys = jnp.where(on_target, positions, positions + entry_count)
    ordered = jnp.argsort(sort_keys)[:capacity]
    counted = jnp.sum(on_target.astype(jnp.int32))
    return (ordered, counted)


def run_blocks(carried, span, step_fn, group_queries, local_flat):
    ordered, counted, first_block, last_block, offset_block, source_tokens, source_lengths = span

    def one_block(block_index, buffers):
        slot_start = block_index * BLOCK
        pos_block = lax.dynamic_slice_in_dim(ordered, slot_start, BLOCK)
        live_block = (slot_start + jnp.arange(BLOCK, dtype=jnp.int32) < counted).astype(jnp.float32)
        local_ids = local_flat[pos_block]
        write_at = (block_index - first_block + offset_block) * BLOCK
        return step_fn(
            buffers,
            write_at,
            pos_block,
            live_block,
            group_queries[pos_block // CAND],
            source_tokens[local_ids],
            source_lengths[local_ids],
        )

    return lax.fori_loop(first_block, last_block, one_block, carried)


def score_step(buffers, write_at, pos_block, live_block, query_rows, passage_rows, lengths):
    slot_pos, slot_scores, slot_live = buffers
    scores, unused = token_softmax(query_rows, passage_rows, lengths)
    return (
        lax.dynamic_update_slice_in_dim(slot_pos, pos_block, write_at, 0),
        lax.dynamic_update_slice_in_dim(slot_scores, scores, write_at, 0),
        lax.dynamic_update_slice_in_dim(slot_live, live_block, write_at, 0),
    )


def body(query_tokens, passage_tokens, passage_lengths, cand_shard, cand_local, teacher_scores):
    group_queries = lax.all_gather(query_tokens, "passage", axis=0, tiled=True)
    own_index = lax.axis_index("passage")
    group_size = cand_local.shape[0]
    shard_rows = passage_tokens.shape[0]
    shard_flat = cand_shard[:, :, 0].reshape(-1)
    local_flat = cand_local.reshape(-1)
    own_order, own_count = shard_slots(shard_flat, own_index, MOST)
    own_blocks = (own_count + BLOCK - 1) // BLOCK
    own_lengths = lax.dynamic_slice_in_dim(passage_lengths, own_index * shard_rows, shard_rows)
    spans = ((own_order, own_count, 0, own_blocks, 0, passage_tokens, own_lengths),)
    carried = (
        jnp.zeros((MOST,), jnp.int32),
        jnp.zeros((MOST,), jnp.float32),
        jnp.zeros((MOST,), jnp.float32),
    )
    span = spans[0]
    carried = run_blocks(carried, span, score_step, group_queries, local_flat)
    slot_pos, slot_scores, slot_live = carried
    teacher_top = jnp.max(teacher_scores, axis=1, keepdims=True)
    log_teacher = teacher_scores - (
        teacher_top + jnp.log(jnp.sum(jnp.exp(teacher_scores - teacher_top), axis=1, keepdims=True))
    )
    teacher_probs = jnp.exp(log_teacher)
    query_total = lax.axis_size("query") * group_size
    dense_scores = (
        jnp.zeros((group_size * CAND,), jnp.float32).at[slot_pos].add(slot_scores * slot_live)
    )
    all_scores = lax.psum(dense_scores.reshape(group_size, CAND), "passage")
    student_top = jnp.max(all_scores, axis=1, keepdims=True)
    log_student = all_scores - (
        student_top + jnp.log(jnp.sum(jnp.exp(all_scores - student_top), axis=1, keepdims=True))
    )
    group_kl = jnp.sum(teacher_probs * (log_teacher - log_student))
    loss = lax.psum(group_kl, "query") / query_total
    coef_dense = (jnp.exp(log_student) - teacher_probs).reshape(-1)
    slot_coef = coef_dense[slot_pos] * slot_live

    def grad_step(
        partial_value, write_at, pos_block, live_block, query_rows, passage_rows, lengths
    ):
        unused, weights = token_softmax(query_rows, passage_rows, lengths)
        pair_grads = jnp.einsum(
            "bij,bjd->bid", weights, passage_rows, preferred_element_type=jnp.float32
        )
        coef_block = lax.dynamic_slice_in_dim(slot_coef, write_at, BLOCK)
        return partial_value.at[pos_block // CAND].add(coef_block[:, None, None] * pair_grads)

    partial_grads = jnp.zeros((group_size,) + query_tokens.shape[1:], jnp.float32)
    span = spans[0]
    partial_grads = run_blocks(partial_grads, span, grad_step, group_queries, local_flat)
    query_grads = lax.psum_scatter(partial_grads, "passage", scatter_dimension=0, tiled=True)
    return (loss, query_grads)


def solution(mesh):
    placed = (
        P(("query", "passage"), None, None),
        P("passage", None, None),
        P(),
        P("query", None, None),
        P("query", None),
        P("query", None),
    )
    return jax.shard_map(
        body,
        mesh=mesh,
        in_specs=placed,
        out_specs=(P(), P(("query", "passage"), None, None)),
        check_vma=False,
    )
```

profile of v0, /device:TPU:1, one launch (start us, length us, event | category | flops | bytes accessed | tf_op | source)
XLA Modules:
  0.0 613.5 jit_solution(8997609337551194719)
XLA Ops:
  7.2 1.5 fusion.12
  9.3 0.9 compare_reduce_fusion
  10.2 0.9 reduce_max.42
  11.1 0.9 exponential_reduce_fusion.1
  12.1 0.8 copy.8
  12.9 6.8 %sort.17 = (s32[8192]{0:T(1024)}, s32[8192]{0:T(1024)S(1)}) sort(s32[8192]{0:T(1024)S(1)} %add_select_fusion, s32[8192]{0:T(1024)S(1)} %iota.39), dimensions={0}, to_apply=%region_3.4 | sort | flops 106496 | bytes 131072 | tf_op jit(solution)/shard_map/jit(argsort)/sort | solution.py:32
  19.6 38.7 %all_gather.3 = bf16[32,32,128]{2,1,0:T(8,128)(2,1)S(1)} all-gather(bf16[1,32,128]{2,1,0:T(8,128)(2,1)} %param.10), channel_id=1, replica_groups=mesh['query'=16,'passage'=32] {'passage'}, dimensions={0}, use_global_device_ids=true | all-gather | bytes 270336 | tf_op jit(solution)/shard_map/all_gather | solution.py:70
  58.3 0.8 dynamic_slice.21
  59.1 26.5 %while.28 = (s32[]{:T(128)}, s32[512]{0:T(512)S(1)}, f32[512]{0:T(512)S(1)}, f32[512]{0:T(512)S(1)}, s32[]{:T(128)}, /*index=5*/s32[512]{0:T(512)S(1)}, s32[8192...) while((s32[]{:T(128)}, s32[512]{0:T(512)S(1)}, ...), condition=%wide.region_8.9_spmd, body=%wide.region_4.8_spmd.sunk | while | flops 138434816 | bytes 28466408 | solution.py:56
  59.1 0.2 compare_select_fusion.15
  59.3 1.1 gather_fusion
  60.5 1.2 gather_fusion.1
  61.8 0.8 gather_fusion.2
  62.6 3.0 gather_fusion.3
  65.6 4.6 fusion.36
  70.2 1.3 select_reduce_fusion.2
  71.6 0.8 fusion.37
  72.4 0.2 compare_select_fusion.15
  72.5 1.1 gather_fusion
  73.7 1.2 gather_fusion.1
  75.1 0.8 gather_fusion.2
  75.8 3.0 gather_fusion.3
  78.8 4.6 fusion.36
  83.4 1.3 select_reduce_fusion.2
  84.8 0.8 fusion.37
  85.6 4.1 scatter_custom_fusion.1
  89.7 130.9 %psum.14 = f32[32,256]{1,0:T(8,128)S(1)} all-reduce(f32[32,256]{1,0:T(8,128)S(1)} %reshape.112), channel_id=1, replica_groups=mesh['query'=16,'passage'=32] {'passage'}, use_global_device_ids=true, to_apply=%region_10.11 | all-reduce | flops 8192 | bytes 65536 | tf_op jit(solution)/shard_map/psum | solution.py:97
  220.8 0.2 exponential_reduce_fusion
  221.0 0.7 subtract_bitcast_fusion
  221.7 3.1 gather_fusion.8
  224.9 62.1 %while.29 = (s32[]{:T(128)}, f32[32,32,128]{2,1,0:T(8,128)S(1)}, s32[]{:T(128)}, s32[512]{0:T(512)S(1)}, f32[512]{0:T(512)S(1)}, /*index=5*/s32[8192]{0:T(1024)S...) while((s32[]{:T(128)}, f32[32,32,128]{2,1,0:T(8,128)S(1)}, ...), condition=%wide.region_19.20_spmd, body=%wide.region_15.19_spmd.sunk | while | flops 273176576 | bytes 32594612 | solution.py:56
  225.3 1.1 gather_fusion.4
  226.5 1.2 gather_fusion.6
  227.8 1.7 gather_fusion.7
  229.5 3.0 gather_fusion.5
  232.5 6.2 %fusion.42 = (f32[128,32]{1,0:T(8,128)S(1)}, f32[128,32,128]{2,1,0:T(8,128)}) fusion(pred[128,128]{1,0:T(8,128)(4,1)S(1)} %iota_compare_fusion.5, bf16[128,32,128]{2,1,0:T(8,128)(2,1)} %gather_fusion.7, bf16[128,128,128]{2,1,0:T(8,128)(2,1)} %gather_fusion.5), kind=kOutput, calls=%fused_computation.69.clone.1 | convolution fusion | flops 136839296 | bytes 7372800 | tf_op jit(solution)/shard_map/while/body/sub | solution.py:20
  238.8 5.5 convolution_multiply_fusion.2
  244.2 11.9 %scatter_fusion = f32[32,32,128]{2,1,0:T(8,128)S(1)} fusion(f32[32,32,128]{2,1,0:T(8,128)S(1)} %get-tuple-element.532, s32[128]{0:T(128)S(1)} %get-tuple-element.467, f32[128,32,128]{2,1,0:T(8,128)} %convolution_multiply_fusion.2), kind=kCustom, calls=%fused_computation.9.clone.1 | custom fusion | flops 524288 | bytes 6291968 | tf_op jit(solution)/shard_map/while/body/scatter-add | solution.py:115
  256.3 1.1 gather_fusion.4
  257.5 1.2 gather_fusion.6
  258.8 1.7 gather_fusion.7
  260.5 3.0 gather_fusion.5
  263.5 6.2 %fusion.42 = (f32[128,32]{1,0:T(8,128)S(1)}, f32[128,32,128]{2,1,0:T(8,128)}) fusion(pred[128,128]{1,0:T(8,128)(4,1)S(1)} %iota_compare_fusion.5, bf16[128,32,128]{2,1,0:T(8,128)(2,1)} %gather_fusion.7, bf16[128,128,128]{2,1,0:T(8,128)(2,1)} %gather_fusion.5), kind=kOutput, calls=%fused_computation.69.clone.1 | convolution fusion | flops 136839296 | bytes 7372800 | tf_op jit(solution)/shard_map/while/body/sub | solution.py:20
  269.7 5.5 convolution_multiply_fusion.2
  275.2 11.9 %scatter_fusion = f32[32,32,128]{2,1,0:T(8,128)S(1)} fusion(f32[32,32,128]{2,1,0:T(8,128)S(1)} %get-tuple-element.532, s32[128]{0:T(128)S(1)} %get-tuple-element.467, f32[128,32,128]{2,1,0:T(8,128)} %convolution_multiply_fusion.2), kind=kCustom, calls=%fused_computation.9.clone.1 | custom fusion | flops 524288 | bytes 6291968 | tf_op jit(solution)/shard_map/while/body/scatter-add | solution.py:115
  287.1 0.8 copy-done.2
  287.9 133.4 %psum.15 = f32[]{:T(128)} all-reduce(f32[]{:T(128)} %get-tuple-element.322), channel_id=1, replica_groups=mesh['query'=16,'passage'=32] {'query'}, use_global_device_ids=true, to_apply=%region_14.15 | all-reduce | flops 1 | bytes 8 | tf_op jit(solution)/shard_map/psum | solution.py:103
  421.9 183.6 %reduce-scatter.2.cloned.1.call-done = f32[1,32,128]{2,1,0:T(8,128)} async-done(((f32[32,32,128]{2,1,0:T(8,128)}), f32[1,32,128]{2,1,0:T(8,128)}) %reduce-scatter.2.cloned.1.call-update) | async-done | bytes 16400 | tf_op jit(solution)/shard_map/reduce_scatter | solution.py:120
  (52 shorter events, 1.3 us)
Async XLA Ops:
  7.2 598.4 %reduce-scatter.2.cloned.1.call-start = ((), (), s32[]{:S(2)}) async-start(), calls=%async_computation.1 | async-start | bytes 540672 | tf_op jit(solution)/shard_map/reduce_scatter | solution.py:120
  59.1 161.9 %copy-start.3 = (f32[32,256]{1,0:T(8,128)S(1)}, f32[32,256]{1,0:T(8,128)}, u32[]{:S(2)}) copy-start(f32[32,256]{1,0:T(8,128)} %param.15) | copy-start | bytes 98308
  59.1 3.5 copy-start
  72.4 3.5 copy-start
  85.6 139.4 %copy-start.1 = (bf16[64,128,128]{2,1,0:T(8,128)(2,1)S(1)}, bf16[64,128,128]{2,1,0:T(8,128)(2,1)}, u32[]{:S(2)}) copy-start(bf16[64,128,128]{2,1,0:T(8,128)(2,1)} %get-tuple-element.560) | copy-start | bytes 6291460
  287.1 0.8 copy-start.2
Sparse Core Ops, SparseCore 0:
  288.0 317.4 reduce-scatter.1
where the time goes:
time: 619 us; the launch traced here: 614 us
  blocking collectives  303 us (49%)
  waiting for transfers between devices  184 us (30%)
  other arithmetic  45 us (7%)
  matrix products  32.5 us (5%)
  local copies, waits for them, and re-layouts  32.2 us (5%)
  between operations  16.6 us (3%)
    reduce_scatter x1, waiting for transfers between devices, body(): lax.psum_scatter(partial_grads, 'passage', scatter_dimension=0, tiled=True)  184 us
    psum x1, blocking collectives, body(): loss = lax.psum(group_kl, 'query') / query_total  133 us
    psum x1, blocking collectives, body(): all_scores = lax.psum(dense_scores.reshape(group_size, CAND), 'passage')  131 us
    all_gather x1, blocking collectives, body(): group_queries = lax.all_gather(query_tokens, 'passage', axis=0, tiled=True)  38.7 us
    scatter-add x2, other arithmetic, grad_step(): partial_value.at[pos_block // CAND]  23.8 us
    sub x2, matrix products, token_softmax(): exp_terms = jnp.where(in_length, jnp.exp(logits - row_top), 0.0)  12.5 us
  transfers between devices with their start and end apart: 1, of which 1 were waited for; matrix products, arithmetic and copies ran while one was open for 0% of the time, Pallas kernels for 0%

commit v1 on v0

v1 whole, which is shorter than its diff:
```python
import functools
import jax
import jax.numpy as jnp
from jax import lax
from jax.experimental import pallas as pl
from jax.experimental.pallas import tpu as pltpu
from jax.sharding import PartitionSpec as P

LANES = 128
SLOTS = 4
UNROLL = 4
FLOOR = -1e30
NT = (((1,), (1,)), ((), ()))
VMEM = pl.BlockSpec(memory_space=pltpu.VMEM)
SMEM = pl.BlockSpec(memory_space=pltpu.SMEM)
f32 = jnp.float32
bf16 = jnp.bfloat16
i32 = jnp.int32


def call(kernel, outs, in_specs, cost, scratch=()):
    return pl.pallas_call(
        kernel,
        out_shape=outs,
        in_specs=in_specs,
        out_specs=tuple(VMEM for _ in outs),
        scratch_shapes=scratch,
        compiler_params=pltpu.CompilerParams(vmem_limit_bytes=32 * 1024 * 1024),
        cost_estimate=pl.CostEstimate(flops=cost, bytes_accessed=cost // 100, transcendentals=0),
    )


def iota(shape, axis):
    return lax.broadcasted_iota(i32, shape, axis)


def plan(me_ref, shard_ref, local_ref, teacher_ref, lengths_ref, table_ref, slots_ref, count_ref, mass_ref, entropy_ref):
    group, passages = shard_ref.shape[0], lengths_ref.shape[1]
    units = table_ref.shape[1]
    teacher = teacher_ref[...]
    top = jnp.max(teacher, axis=1, keepdims=True)
    log_teacher = teacher - (top + jnp.log(jnp.sum(jnp.exp(teacher - top), axis=1, keepdims=True)))
    probs = jnp.exp(log_teacher)
    entropy_ref[...] = jnp.broadcast_to(jnp.sum(probs * log_teacher, keepdims=True), entropy_ref.shape)
    key = jnp.where(shard_ref[...] == me_ref[0], local_ref[...], -1)
    row = iota((passages, key.shape[1]), 0)
    lane = iota((passages, LANES), 1)
    count = jnp.zeros((passages, LANES), f32)
    mass = jnp.zeros((passages, LANES), f32)
    for q in range(group):
        hit = key[q : q + 1, :] == row
        count = jnp.where(lane == q, jnp.sum(jnp.where(hit, 1.0, 0.0), axis=1, keepdims=True), count)
        mass = jnp.where(lane == q, jnp.sum(jnp.where(hit, probs[q : q + 1, :], 0.0), axis=1, keepdims=True), mass)
    count_ref[...] = count
    mass_ref[...] = mass
    live = count > 0.0
    live_b = jnp.where(live, 1.0, 0.0).astype(bf16)
    before = jnp.where(iota((LANES, LANES), 0) < iota((LANES, LANES), 1), 1.0, 0.0).astype(bf16)
    rank = jnp.dot(live_b, before, preferred_element_type=f32)
    rank = jnp.where(live, rank, -1.0)
    named = lax.dot_general(jnp.ones((8, LANES), bf16), live_b, NT, preferred_element_type=f32)
    needed = ((named.astype(i32) + (SLOTS - 1)) // SLOTS).astype(f32)
    before_p = jnp.where(iota((passages, passages), 0) < iota((passages, passages), 1), 1.0, 0.0).astype(bf16)
    first = jnp.dot(needed.astype(bf16), before_p, preferred_element_type=f32)
    needed, first = needed[0:1, :], first[0:1, :]
    total = jnp.sum(needed, axis=1, keepdims=True)
    unit = iota((units, passages), 0).astype(f32)
    own = (unit >= first) & (unit < first + needed)
    own_f = jnp.where(own, 1.0, 0.0)
    own_b = own_f.astype(bf16)
    passage = jnp.sum(jnp.where(own, iota((units, passages), 1).astype(f32), 0.0), axis=1, keepdims=True)
    length = jnp.sum(jnp.where(own, lengths_ref[...].astype(f32), 0.0), axis=1, keepdims=True)
    offset = jnp.sum(jnp.where(own, unit - first, 0.0), axis=1, keepdims=True) * SLOTS
    wide = iota((units, LANES), 1)
    used = iota((units, LANES), 0).astype(f32) < total
    unit_rank = jnp.where(used, jnp.dot(own_b, rank.astype(bf16), preferred_element_type=f32), -1.0)
    unit_count = jnp.dot(own_b, count.astype(bf16), preferred_element_type=f32)
    unit_mass = jnp.dot(own_f, mass, preferred_element_type=f32, precision=lax.Precision.HIGHEST)
    ints = jnp.where(wide == SLOTS, passage, 0.0)
    ints = jnp.where(wide == SLOTS + 1, length, ints)
    ints = jnp.where(wide == SLOTS + 2, total, ints)
    floats = jnp.zeros((units, LANES), f32)
    wide_f = wide.astype(f32)
    for k in range(SLOTS):
        pick = unit_rank == offset + float(k)
        query = group + jnp.sum(jnp.where(pick, wide_f - group, 0.0), axis=1, keepdims=True)
        ints = jnp.where(wide == k, query, ints)
        floats = jnp.where(wide == k, jnp.sum(jnp.where(pick, unit_count, 0.0), axis=1, keepdims=True), floats)
        floats = jnp.where(wide == SLOTS + k, jnp.sum(jnp.where(pick, unit_mass, 0.0), axis=1, keepdims=True), floats)
    table_ref[...] = jnp.transpose(ints)[: table_ref.shape[0], :].astype(i32)
    slots_ref[...] = jnp.transpose(floats)[: slots_ref.shape[0], :]


def trips(table_ref):
    return (table_ref[SLOTS + 2, 0] + (UNROLL - 1)) // UNROLL


def score(table_ref, query_ref, passage_ref, count_ref, mass_ref, weight_ref, slot_score_ref, local_ref, top_ref, dense_ref):
    group, qlen = query_ref.shape[0], query_ref.shape[1]
    rows, plen = SLOTS * qlen, passage_ref.shape[1]
    dense_ref[...] = jnp.zeros(dense_ref.shape, f32)
    lane = iota((1, LANES), 1)
    column = iota((rows, plen), 1)

    def one(u):
        p, length = table_ref[SLOTS, u], table_ref[SLOTS + 1, u]
        queries = [table_ref[k, u] for k in range(SLOTS)]
        tokens = jnp.concatenate([query_ref[jnp.minimum(q, group - 1)] for q in queries], axis=0)
        logits = lax.dot_general(tokens, passage_ref[p], NT, preferred_element_type=f32)
        logits = jnp.where(column < length, logits, FLOOR)
        top = jnp.max(logits, axis=1, keepdims=True)
        terms = jnp.exp(logits - top)
        total = jnp.sum(terms, axis=1, keepdims=True)
        weight_ref[u] = (terms * (1.0 / total)).astype(bf16)
        tops = jnp.broadcast_to(top, (rows, LANES)).reshape(SLOTS, qlen // 8, 8, LANES)
        totals = jnp.broadcast_to(total, (rows, LANES)).reshape(SLOTS, qlen // 8, 8, LANES)
        sum_top, product = tops[:, 0], totals[:, 0]
        for j in range(1, qlen // 8):
            sum_top, product = sum_top + tops[:, j], product * totals[:, j]
        scores = jnp.sum(sum_top + jnp.log(product), axis=1) * 0.5
        slot_score_ref[u] = scores
        dense = dense_ref[pl.ds(p, 1), :]
        for k in range(SLOTS):
            dense = jnp.where(lane == queries[k], scores[k : k + 1, :], dense)
        dense_ref[pl.ds(p, 1), :] = dense

    def some(t, carry):
        for j in range(UNROLL):
            one(t * UNROLL + j)
        return carry

    lax.fori_loop(0, trips(table_ref), some, 0)
    scores, count, mass = dense_ref[...], count_ref[...], mass_ref[...]
    live = count > 0.0
    top = jnp.max(jnp.where(live, scores, FLOOR), axis=0, keepdims=True)
    gap = jnp.where(live, scores - top, 0.0)
    total = jnp.sum(jnp.where(live, count * jnp.exp(gap), 0.0), axis=0, keepdims=True)
    cross = jnp.sum(mass * gap, axis=0, keepdims=True)
    held = jnp.sum(mass, axis=0, keepdims=True)
    packed = jnp.where(lane < group, top, 0.0)
    for k, part in enumerate((total, cross, held)):
        moved = pltpu.roll(jnp.broadcast_to(part, (8, LANES)), (k + 1) * group, 1)[0:1]
        packed = jnp.where(lane // group == k + 1, moved, packed)
    local_ref[...] = jnp.broadcast_to(packed, local_ref.shape)
    top_ref[...] = jnp.transpose(jnp.broadcast_to(top, (LANES, LANES)))


def terms_of(table_ref, slots_ref, weight_ref, passage_ref, slot_score_ref, top_ref, sums_ref):
    qlen = sums_ref.shape[1] // 2
    sums_ref[...] = jnp.zeros(sums_ref.shape, f32)

    def one(u):
        p = table_ref[SLOTS, u]
        grads = jnp.dot(weight_ref[u], passage_ref[p], preferred_element_type=f32)
        queries = [table_ref[k, u] for k in range(SLOTS)]
        olds = [sums_ref[q] for q in queries]
        for k, q in enumerate(queries):
            part = grads[k * qlen : (k + 1) * qlen]
            student = jnp.exp(slot_score_ref[u, k : k + 1, :] - top_ref[pl.ds(q, 1), :]) * slots_ref[k, u]
            sums_ref[q] = olds[k] + jnp.concatenate([student * part, slots_ref[SLOTS + k, u] * part], axis=0)

    def some(t, carry):
        for j in range(UNROLL):
            one(t * UNROLL + j)
        return carry

    lax.fori_loop(0, trips(table_ref), some, 0)


def join(parts_ref, local_ref, entropy_ref, sums_ref, grads_ref, loss_ref):
    group, qlen = grads_ref.shape[0], grads_ref.shape[1]
    parts = parts_ref[...]
    lane = iota((1, LANES), 1)
    total, cross, held = (pltpu.roll(parts, LANES - (k + 1) * group, 1) for k in range(3))
    top = jnp.max(parts, axis=0, keepdims=True)
    lse = top + jnp.log(jnp.sum(total * jnp.exp(parts - top), axis=0, keepdims=True))
    agreed = jnp.sum(cross + held * (parts - lse), axis=0, keepdims=True)
    agreed = jnp.sum(jnp.where(lane < group, agreed, 0.0), axis=1, keepdims=True)
    loss_ref[...] = jnp.broadcast_to(entropy_ref[...] - agreed, loss_ref.shape)
    factor = jnp.where(lane < group, jnp.exp(local_ref[0:1, :] - lse), 0.0)
    factors = jnp.transpose(jnp.broadcast_to(factor, (LANES, LANES)))
    for q in range(group):
        grads_ref[q] = sums_ref[q, :qlen] * factors[q : q + 1, :] - sums_ref[q, qlen:]


def body(query_tokens, passage_tokens, passage_lengths, cand_shard, cand_local, teacher_scores):
    shards, groups = lax.axis_size("passage"), lax.axis_size("query")
    me = lax.axis_index("passage")
    group, cands = cand_local.shape
    qlen, dim = query_tokens.shape[1:]
    passages, plen, _ = passage_tokens.shape
    units = 176
    padded = 256
    doubled = jnp.broadcast_to(query_tokens * 2, (shards, qlen, dim))
    queries = lax.all_to_all(doubled, "passage", 0, 0, tiled=True)
    lengths = lax.dynamic_slice_in_dim(passage_lengths, me * passages, passages).reshape(1, passages)
    table, slots, count, mass, entropy = call(
        plan,
        (
            jax.ShapeDtypeStruct((16, padded), i32),
            jax.ShapeDtypeStruct((8, padded), f32),
            jax.ShapeDtypeStruct((passages, LANES), f32),
            jax.ShapeDtypeStruct((passages, LANES), f32),
            jax.ShapeDtypeStruct((1, LANES), f32),
        ),
        [SMEM, VMEM, VMEM, VMEM, VMEM],
        int(2e9),
    )(me.reshape(1), cand_shard.reshape(group, cands), cand_local, teacher_scores, lengths)
    weights, slot_scores, local, tops = call(
        score,
        (
            jax.ShapeDtypeStruct((units, SLOTS * qlen, plen), bf16),
            jax.ShapeDtypeStruct((units, SLOTS, LANES), f32),
            jax.ShapeDtypeStruct((8, LANES), f32),
            jax.ShapeDtypeStruct((LANES, LANES), f32),
        ),
        [SMEM, VMEM, VMEM, VMEM, VMEM],
        int(4e9),
        [pltpu.VMEM((passages, LANES), f32)],
    )(table, queries, passage_tokens, count, mass)
    parts = lax.all_to_all(jnp.broadcast_to(local[None, 0:1], (shards, 1, LANES)), "passage", 0, 0, tiled=True)
    (sums,) = call(
        terms_of,
        (jax.ShapeDtypeStruct((group + 1, 2 * qlen, dim), f32),),
        [SMEM, SMEM, VMEM, VMEM, VMEM, VMEM],
        int(4e9),
    )(table, slots, weights, passage_tokens, slot_scores, tops)
    grads, loss = call(
        join,
        (jax.ShapeDtypeStruct((group, qlen, dim), f32), jax.ShapeDtypeStruct((1, LANES), f32)),
        [VMEM, VMEM, VMEM, VMEM],
        int(1e9),
    )(parts.reshape(shards, LANES), local, entropy, sums)
    sent = lax.all_to_all(grads, "passage", 0, 0, tiled=True)
    losses = lax.all_to_all(jnp.broadcast_to(loss[None], (groups, 1, LANES)), "query", 0, 0, tiled=True)
    query_grads = jnp.sum(sent, axis=0, keepdims=True)
    return (jnp.sum(losses[:, 0, 0]) / (groups * group), query_grads)


def solution(mesh):
    placed = (
        P(("query", "passage"), None, None),
        P("passage", None, None),
        P(),
        P("query", None, None),
        P("query", None),
        P("query", None),
    )
    return jax.shard_map(
        body,
        mesh=mesh,
        in_specs=placed,
        out_specs=(P(), P(("query", "passage"), None, None)),
        check_vma=False,
    )
```

time: 619 us -> 110 us (0.18)
  blocking collectives: 303 us -> 20.1 us
  waiting for transfers between devices: 184 us -> 22.4 us
  other arithmetic: 45 us -> 1.97 us
  starting transfers between devices: 0.04 us -> 37.2 us
  matrix products: 32.5 us -> 0 us
  local copies, waits for them, and re-layouts: 32.2 us -> 11.3 us
  between operations: 16.6 us -> 2.51 us
  Pallas kernels: 0 us -> 12.9 us
    psum x2 -> x0, blocking collectives: 264 us -> none  [the longest x1 133 us: body(): loss = lax.psum(group_kl, 'query') / query_total]
    reduce_scatter x1 -> x0, waiting for transfers between devices: 184 us -> none  [body(): lax.psum_scatter(partial_grads, 'passage', scatter_dimension=0, tiled=True)]
    all_gather x1 -> x0, blocking collectives: 38.7 us -> none  [body(): group_queries = lax.all_gather(query_tokens, 'passage', axis=0, tiled=True)]
    all_to_all x0 -> x3, starting transfers between devices: none -> 37.2 us  [the longest x1 13.9 us: body(): lax.all_to_all(jnp.broadcast_to(local[None, 0:1], (shards, 1, LANES)), 'p...]
    gather x17 -> x0, local copies, waits for them, and re-layouts: 29.6 us -> none  [the longest x4 12 us: one_block(): source_tokens[local_ids]]
    scatter-add x3 -> x0, other arithmetic: 27.8 us -> none  [the longest x2 23.8 us: grad_step(): partial_value.at[pos_block // CAND]]
    all_to_all x0 -> x3, waiting for transfers between devices: none -> 22.4 us  [the longest x1 15 us: body(): sent = lax.all_to_all(grads, 'passage', 0, 0, tiled=True)]
    all_to_all x0 -> x1, blocking collectives: none -> 20.1 us  [body(): lax.all_to_all(jnp.broadcast_to(loss[None], (groups, 1, LANES)), 'query',...]
  transfers between devices with their start and end apart: 1 -> 3, of which waited for: 1 -> 3; matrix products, arithmetic and copies ran while one was open for 0% -> 1% of each run, Pallas kernels for 0% -> 5%
where the time goes in v1:
time: 110 us; the launch traced here: 108 us
  starting transfers between devices  37.2 us (34%)
  waiting for transfers between devices  22.4 us (20%)
  blocking collectives  20.1 us (18%)
  Pallas kernels  12.9 us (12%)
  local copies, waits for them, and re-layouts  11.3 us (10%)
  between operations  2.51 us (2%)
  other arithmetic  1.97 us (2%)
    all_to_all x1, blocking collectives, body(): lax.all_to_all(jnp.broadcast_to(loss[None], (groups, 1, LANES)), 'query',...  20.1 us
    all_to_all x1, waiting for transfers between devices, body(): sent = lax.all_to_all(grads, 'passage', 0, 0, tiled=True)  15 us
    all_to_all x1, starting transfers between devices, body(): lax.all_to_all(jnp.broadcast_to(local[None, 0:1], (shards, 1, LANES)), 'p...  13.9 us
    all_to_all x1, starting transfers between devices, body(): sent = lax.all_to_all(grads, 'passage', 0, 0, tiled=True)  12.8 us
    all_to_all x1, starting transfers between devices, body(): queries = lax.all_to_all(doubled, 'passage', 0, 0, tiled=True)  10.5 us
    unnamed x25, local copies, waits for them, and re-layouts  9.84 us
    all_to_all x1, waiting for transfers between devices, body(): queries = lax.all_to_all(doubled, 'passage', 0, 0, tiled=True)  7.07 us
    pallas_call x1, Pallas kernels, body(): call(score, (jax.ShapeDtypeStruct((units, SLOTS * qlen, plen), bf16), jax...  6.31 us
  transfers between devices with their start and end apart: 3, of which 3 were waited for; matrix products, arithmetic and copies ran while one was open for 1% of the time, Pallas kernels for 5%

profile of v1, /device:TPU:1, one launch (start us, length us, event | category | flops | bytes accessed | tf_op | source)
XLA Modules:
  0.0 108.4 jit_solution(12510579136786068462)
XLA Ops:
  0.6 0.0 copy-start
  0.6 0.7 multiply_bitcast_fusion
  1.4 0.7 broadcast_in_dim.27
  2.1 10.5 %all-to-all-start = ((bf16[32,32,128]{2,1,0:T(8,128)(2,1)}), bf16[32,32,128]{2,1,0:T(8,128)(2,1)S(1)}, u32[]{:S(2)}, u32[]{:S(2)}) async-start(bf16[32,32,128]{2,1,0:T(8,128)(2,1)} %broadcast_in_dim.27), calls=%async_computation | async-start | bytes 524288 | tf_op jit(solution)/shard_map/all_to_all | solution.py:195
  12.6 0.8 copy.12
  13.4 0.0 copy-done
  13.4 0.1 dynamic-slice_bitcast_fusion.lengths_ref
  13.4 0.0 copy-start.2
  13.4 0.8 copy-done.2
  14.2 0.0 copy-start.3
  14.2 0.8 copy-done.3
  15.0 0.0 copy-start.1
  15.0 1.7 %shard_map.77 = (s32[16,256]{1,0:T(8,128)S(1)}, f32[8,256]{1,0:T(8,128)S(1)}, f32[64,128]{1,0:T(8,128)S(1)}, f32[64,128]{1,0:T(8,128)S(1)}, f32[1,128]{1,0:T(1,128)S(1)}) custom-call(s32[1]{0:T(128)} %bitcast.me_ref, s32[32,256]{1,0:T(8,128)S(1)} %bitcast.13, s32[32,256]{1,0:T(8,128)S(1)} %copy-done.2, f32[32,256]{1,0:T(8,128)S(1)} %copy-done.3, ...), custom_call_target="tpu_custom_call" | custom-call | flops 2000000000 | bytes 20000000 | tf_op jit(solution)/shard_map/pallas_call | solution.py:197
  16.7 0.0 copy-start.8
  16.7 0.0 copy-start.10
  16.7 7.1 %all-to-all-done.query_ref = bf16[32,32,128]{2,1,0:T(8,128)(2,1)S(1)} async-done(((bf16[32,32,128]{2,1,0:T(8,128)(2,1)}), bf16[32,32,128]{2,1,0:T(8,128)(2,1)S(1)}, u32[]{:S(2)}, u32[]{:S(2)}) %all-to-all-start) | async-done | bytes 262176 | tf_op jit(solution)/shard_map/all_to_all | solution.py:195
  23.8 0.0 copy-done.1
  23.8 6.3 %shard_map.78 = (bf16[176,128,128]{2,1,0:T(8,128)(2,1)S(1)}, f32[176,4,128]{2,1,0:T(4,128)S(1)}, f32[8,128]{1,0:T(8,128)S(1)}, f32[128,128]{1,0:T(8,128)S(1)}) custom-call(s32[16,256]{1,0:T(8,128)S(1)} %get-tuple-element.13.table_ref, bf16[32,32,128]{2,1,0:T(8,128)(2,1)S(1)} %all-to-all-done.query_ref, bf16[64,128,128]{2,1,0:T(8,128)(2,1)S(1)} %copy-done.1, ...), custom_call_target="tpu_custom_call" | custom-call | flops 4000000000 | bytes 40000000 | tf_op jit(solution)/shard_map/pallas_call | solution.py:209
  30.1 0.0 copy-done.8
  30.1 0.0 copy-done.10
  30.1 0.0 copy-start.4
  30.1 2.5 %copy-done.4 = bf16[176,128,128]{2,1,0:T(8,128)(2,1)} copy-done((bf16[176,128,128]{2,1,0:T(8,128)(2,1)}, bf16[176,128,128]{2,1,0:T(8,128)(2,1)S(1)}, u32[]{:S(2)}) %copy-start.4) | copy-done | bytes 5767192
  32.6 0.0 copy-start.6
  32.6 0.7 copy-done.6
  33.3 0.6 broadcast_in_dim.29
  34.0 13.9 %all-to-all-start.1 = ((f32[32,1,128]{2,1,0:T(1,128)}), f32[32,1,128]{2,1,0:T(1,128)S(1)}, u32[]{:S(2)}, u32[]{:S(2)}) async-start(f32[32,1,128]{2,1,0:T(1,128)} %broadcast_in_dim.29), calls=%async_computation.1 | async-start | bytes 32768 | tf_op jit(solution)/shard_map/all_to_all | solution.py:221
  47.9 0.0 copy-start.5
  47.9 2.6 %copy-done.5 = bf16[176,128,128]{2,1,0:T(8,128)(2,1)S(1)} copy-done((bf16[176,128,128]{2,1,0:T(8,128)(2,1)S(1)}, bf16[176,128,128]{2,1,0:T(8,128)(2,1)}, u32[]{:S(2)}) %copy-start.5) | copy-done | bytes 5767192
  50.5 0.0 copy-start.7
  50.5 1.0 copy-done.7
  51.5 0.0 copy-start.9
  51.5 0.7 copy-done.9
  52.2 0.0 copy-start.11
  52.2 3.8 %shard_map.79.sums_ref = f32[33,64,128]{2,1,0:T(8,128)S(1)} custom-call(s32[16,256]{1,0:T(8,128)S(1)} %copy-done.9, f32[8,256]{1,0:T(8,128)S(1)} %get-tuple-element.18.slots_ref, bf16[176,128,128]{2,1,0:T(8,128)(2,1)S(1)} %copy-done.5, bf16[64,128,128]{2,1,0:T(8,128)(2,1)S(1)} %copy-done.1, f32[176,4,128]{2,1,0:T(4,128)S(1)} %copy-done.7, ...), custom_call_target="tpu_custom_call" | custom-call | flops 4000000000 | bytes 40000000 | tf_op jit(solution)/shard_map/pallas_call | solution.py:222
  56.1 0.3 all-to-all-done.1
  56.4 0.0 copy-done.11
  56.4 1.0 shard_map.80
  57.4 20.1 %all_to_all.20 = f32[16,1,128]{2,1,0:T(1,128)S(1)} all-to-all(f32[16,1,128]{2,1,0:T(1,128)S(1)} %broadcast_in_dim.31), channel_id=1, replica_groups=mesh['query'=16,'passage'=32] {'query'}, dimensions={0} | all-to-all | bytes 16384 | tf_op jit(solution)/shard_map/all_to_all | solution.py:235
  77.5 12.8 %all-to-all-start.3 = ((f32[32,32,128]{2,1,0:T(8,128)}), f32[32,32,128]{2,1,0:T(8,128)S(1)}, u32[]{:S(2)}, u32[]{:S(2)}) async-start(f32[32,32,128]{2,1,0:T(8,128)} %get-tuple-element.23), calls=%async_computation.3 | async-start | bytes 1048576 | tf_op jit(solution)/shard_map/all_to_all | solution.py:234
  90.3 0.6 slice_reduce_fusion
  91.6 15.0 %all-to-all-done.3 = f32[32,32,128]{2,1,0:T(8,128)S(1)} async-done(((f32[32,32,128]{2,1,0:T(8,128)}), f32[32,32,128]{2,1,0:T(8,128)S(1)}, u32[]{:S(2)}, u32[]{:S(2)}) %all-to-all-start.3) | async-done | bytes 524320 | tf_op jit(solution)/shard_map/all_to_all | solution.py:234
  106.6 0.6 reduce_sum.19
  (2 shorter events, 0.0 us)
Async XLA Ops:
  0.6 12.7 %copy-start = (s32[2048]{0:T(1024)S(1)}, s32[2048]{0:T(1024)}, u32[]{:S(2)}) copy-start(s32[2048]{0:T(1024)} %param.8) | copy-start | bytes 24580
  2.1 21.7 %all-to-all-start = ((bf16[32,32,128]{2,1,0:T(8,128)(2,1)}), bf16[32,32,128]{2,1,0:T(8,128)(2,1)S(1)}, u32[]{:S(2)}, u32[]{:S(2)}) async-start(bf16[32,32,128]{2,1,0:T(8,128)(2,1)} %broadcast_in_dim.27), calls=%async_computation | async-start | bytes 524288 | tf_op jit(solution)/shard_map/all_to_all | solution.py:195
  13.4 0.8 copy-start.2
  14.2 0.8 copy-start.3
  15.0 8.8 %copy-start.1 = (bf16[64,128,128]{2,1,0:T(8,128)(2,1)S(1)}, bf16[64,128,128]{2,1,0:T(8,128)(2,1)}, u32[]{:S(2)}) copy-start(bf16[64,128,128]{2,1,0:T(8,128)(2,1)} %passage_ref.3) | copy-start | bytes 6291460
  16.7 13.4 %copy-start.8 = (s32[16,256]{1,0:T(8,128)}, s32[16,256]{1,0:T(8,128)S(1)}, u32[]{:S(2)}) copy-start(s32[16,256]{1,0:T(8,128)S(1)} %get-tuple-element.13.table_ref) | copy-start | bytes 49156
  16.7 13.4 %copy-start.10 = (f32[1,128]{1,0:T(1,128)}, f32[1,128]{1,0:T(1,128)S(1)}, u32[]{:S(2)}) copy-start(f32[1,128]{1,0:T(1,128)S(1)} %get-tuple-element.17.entropy_ref) | copy-start | bytes 1540
  30.1 2.5 %copy-start.4 = (bf16[176,128,128]{2,1,0:T(8,128)(2,1)}, bf16[176,128,128]{2,1,0:T(8,128)(2,1)S(1)}, u32[]{:S(2)}) copy-start(bf16[176,128,128]{2,1,0:T(8,128)(2,1)S(1)} %get-tuple-element.19.weight_ref) | copy-start | bytes 17301508
  32.6 0.7 copy-start.6
  34.0 22.4 %all-to-all-start.1 = ((f32[32,1,128]{2,1,0:T(1,128)}), f32[32,1,128]{2,1,0:T(1,128)S(1)}, u32[]{:S(2)}, u32[]{:S(2)}) async-start(f32[32,1,128]{2,1,0:T(1,128)} %broadcast_in_dim.29), calls=%async_computation.1 | async-start | bytes 32768 | tf_op jit(solution)/shard_map/all_to_all | solution.py:221
  47.9 2.6 %copy-start.5 = (bf16[176,128,128]{2,1,0:T(8,128)(2,1)S(1)}, bf16[176,128,128]{2,1,0:T(8,128)(2,1)}, u32[]{:S(2)}) copy-start(bf16[176,128,128]{2,1,0:T(8,128)(2,1)} %copy-done.4) | copy-start | bytes 17301508
  50.5 1.0 copy-start.7
  51.5 0.7 copy-start.9
  52.2 4.2 %copy-start.11 = (f32[1,128]{1,0:T(1,128)S(1)}, f32[1,128]{1,0:T(1,128)}, u32[]{:S(2)}) copy-start(f32[1,128]{1,0:T(1,128)} %copy-done.10) | copy-start | bytes 1540
  77.5 29.1 %all-to-all-start.3 = ((f32[32,32,128]{2,1,0:T(8,128)}), f32[32,32,128]{2,1,0:T(8,128)S(1)}, u32[]{:S(2)}, u32[]{:S(2)}) async-start(f32[32,32,128]{2,1,0:T(8,128)} %get-tuple-element.23), calls=%async_computation.3 | async-start | bytes 1048576 | tf_op jit(solution)/shard_map/all_to_all | solution.py:234

commit v2 on v1

v2 whole, which is shorter than its diff:
```python
import jax
import jax.numpy as jnp
from jax import lax
from jax.experimental import pallas as pl
from jax.experimental.pallas import tpu as pltpu
from jax.sharding import PartitionSpec as P

LANES = 128
SLOTS = 4
UNROLL = 4
FLOOR = -1e30
NT = (((1,), (1,)), ((), ()))
VMEM = pl.BlockSpec(memory_space=pltpu.VMEM)
HBM = pl.BlockSpec(memory_space=pltpu.HBM)
SMEM = pl.BlockSpec(memory_space=pltpu.SMEM)
f32 = jnp.float32
bf16 = jnp.bfloat16
i32 = jnp.int32


def held(shape, dtype):
    return pltpu.VMEM(shape, dtype)


def call(kernel, outs, in_specs, cost, scratch=()):
    return pl.pallas_call(
        kernel,
        out_shape=outs,
        in_specs=in_specs,
        out_specs=tuple(HBM if getattr(o, "memory_space", None) == pltpu.HBM else VMEM for o in outs),
        scratch_shapes=scratch,
        compiler_params=pltpu.CompilerParams(vmem_limit_bytes=24 * 1024 * 1024),
        cost_estimate=pl.CostEstimate(flops=cost, bytes_accessed=cost // 100, transcendentals=0),
    )


def iota(shape, axis):
    return lax.broadcasted_iota(i32, shape, axis)


def plan(me_ref, shard_ref, local_ref, teacher_ref, lengths_ref, table_ref, slot_ref, count_ref, mass_ref, entropy_ref):
    group, passages = shard_ref.shape[0], lengths_ref.shape[1]
    units, padded = count_ref.shape[0], table_ref.shape[1]
    teacher = teacher_ref[...]
    top = jnp.max(teacher, axis=1, keepdims=True)
    log_teacher = teacher - (top + jnp.log(jnp.sum(jnp.exp(teacher - top), axis=1, keepdims=True)))
    probs = jnp.exp(log_teacher)
    entropy_ref[...] = jnp.broadcast_to(jnp.sum(probs * log_teacher, keepdims=True), entropy_ref.shape)
    key = jnp.where(shard_ref[...] == me_ref[0], local_ref[...], -1)
    row = iota((passages, key.shape[1]), 0)
    lane = iota((passages, LANES), 1)
    count = jnp.zeros((passages, LANES), f32)
    mass = jnp.zeros((passages, LANES), f32)
    for q in range(group):
        hit = key[q : q + 1, :] == row
        count = jnp.where(lane == q, jnp.sum(jnp.where(hit, 1.0, 0.0), axis=1, keepdims=True), count)
        mass = jnp.where(lane == q, jnp.sum(jnp.where(hit, probs[q : q + 1, :], 0.0), axis=1, keepdims=True), mass)
    live = count > 0.0
    live_b = jnp.where(live, 1.0, 0.0).astype(bf16)
    before = jnp.where(iota((LANES, LANES), 0) < iota((LANES, LANES), 1), 1.0, 0.0).astype(bf16)
    rank = jnp.dot(live_b, before, preferred_element_type=f32)
    rank = jnp.where(live, rank, -1.0)
    named = lax.dot_general(jnp.ones((8, LANES), bf16), live_b, NT, preferred_element_type=f32)
    needed = ((named.astype(i32) + (SLOTS - 1)) // SLOTS).astype(f32)
    before_p = jnp.where(iota((passages, passages), 0) < iota((passages, passages), 1), 1.0, 0.0).astype(bf16)
    first = jnp.dot(needed.astype(bf16), before_p, preferred_element_type=f32)
    needed, first = needed[0:1, :], first[0:1, :]
    total = jnp.sum(needed, axis=1, keepdims=True)
    unit = iota((padded, passages), 0).astype(f32)
    own = (unit >= first) & (unit < first + needed)
    own_f = jnp.where(own, 1.0, 0.0)
    own_b = own_f.astype(bf16)
    passage = jnp.sum(jnp.where(own, iota((padded, passages), 1).astype(f32), 0.0), axis=1, keepdims=True)
    length = jnp.sum(jnp.where(own, lengths_ref[...].astype(f32), 0.0), axis=1, keepdims=True)
    offset = jnp.sum(jnp.where(own, unit - first, 0.0), axis=1, keepdims=True) * SLOTS
    wide = iota((padded, LANES), 1)
    used = iota((padded, LANES), 0).astype(f32) < total
    unit_rank = jnp.dot(own_b, rank.astype(bf16), preferred_element_type=f32)
    slot = jnp.where(used & (unit_rank >= 0.0), unit_rank - offset, -1.0)
    here = (slot >= 0.0) & (slot < float(SLOTS))
    slot = jnp.where(here, slot, -1.0)
    unit_count = jnp.where(here, jnp.dot(own_b, count.astype(bf16), preferred_element_type=f32), 0.0)
    unit_mass = jnp.dot(own_f, mass, preferred_element_type=f32, precision=lax.Precision.HIGHEST)
    unit_mass = jnp.where(here, unit_mass, 0.0)
    slot_ref[...] = slot[:units]
    count_ref[...] = unit_count[:units]
    mass_ref[...] = unit_mass[:units]
    ints = jnp.where(wide == SLOTS, passage, 0.0)
    ints = jnp.where(wide == SLOTS + 1, length, ints)
    ints = jnp.where(wide == SLOTS + 2, total, ints)
    wide_f = wide.astype(f32)
    for k in range(SLOTS):
        pick = slot == float(k)
        query = group + jnp.sum(jnp.where(pick, wide_f - group, 0.0), axis=1, keepdims=True)
        ints = jnp.where(wide == k, query, ints)
    table_ref[...] = jnp.transpose(ints)[: table_ref.shape[0], :].astype(i32)


def trips(table_ref):
    return (table_ref[SLOTS + 2, 0] + (UNROLL - 1)) // UNROLL


def score(table_ref, query_ref, passage_ref, slot_ref, count_ref, mass_ref, weight_ref, student_ref, local_ref, double_ref, row_ref, buffer_ref, sems):
    group, qlen = query_ref.shape[0], query_ref.shape[1]
    units, plen, columns = weight_ref.shape
    double_ref[...] = query_ref[...] * 2
    row_ref[...] = jnp.zeros(row_ref.shape, f32)
    position = iota((plen, columns), 0)
    rounds = trips(table_ref)

    def out(t):
        return pltpu.make_async_copy(buffer_ref.at[t % 2], weight_ref.at[pl.ds(t * UNROLL, UNROLL)], sems.at[t % 2])

    def some(t, carry):
        @pl.when(t >= 2)
        def _():
            out(t - 2).wait()

        for j in range(UNROLL):
            u = t * UNROLL + j
            p, length = table_ref[SLOTS, u], table_ref[SLOTS + 1, u]
            tokens = jnp.concatenate([double_ref[jnp.minimum(table_ref[k, u], group - 1)] for k in range(SLOTS)], axis=0)
            logits = lax.dot_general(passage_ref[p], tokens, NT, preferred_element_type=f32)
            logits = jnp.where(position < length, logits, FLOOR)
            top = jnp.max(logits, axis=0, keepdims=True)
            terms = jnp.exp(logits - top)
            total = jnp.sum(terms, axis=0, keepdims=True)
            buffer_ref[t % 2, j] = (terms * (1.0 / total)).astype(bf16)
            row_ref[pl.ds(u, 1), :] = top + jnp.log(total)
        out(t).start()
        return carry

    lax.fori_loop(0, rounds, some, 0)
    for back in (2, 1):

        @pl.when(rounds >= back)
        def _():
            out(rounds - back).wait()

    same = iota((columns, LANES), 0) // qlen == iota((columns, LANES), 1)
    summed = jnp.dot(row_ref[...], jnp.where(same, 0.5, 0.0), preferred_element_type=f32, precision=lax.Precision.HIGHEST)
    slot, count, mass = slot_ref[...], count_ref[...], mass_ref[...]
    scores = jnp.zeros((units, LANES), f32)
    for k in range(SLOTS):
        scores = jnp.where(slot == float(k), jnp.broadcast_to(summed[:, k : k + 1], (units, LANES)), scores)
    live = slot >= 0.0
    top = jnp.max(jnp.where(live, scores, FLOOR), axis=0, keepdims=True)
    gap = jnp.where(live, scores - top, 0.0)
    student = jnp.where(live, count * jnp.exp(gap), 0.0)
    student_ref[...] = student
    total = jnp.sum(student, axis=0, keepdims=True)
    cross = jnp.sum(mass * gap, axis=0, keepdims=True)
    kept = jnp.sum(mass, axis=0, keepdims=True)
    lane = iota((1, LANES), 1)
    packed = jnp.where(lane < group, top, 0.0)
    for k, part in enumerate((total, cross, kept)):
        moved = pltpu.roll(jnp.broadcast_to(part, (8, LANES)), (k + 1) * group, 1)[0:1]
        packed = jnp.where(lane // group == k + 1, moved, packed)
    local_ref[...] = jnp.broadcast_to(packed, local_ref.shape)


def terms_of(table_ref, weight_ref, passage_ref, slot_ref, student_ref, mass_ref, sums_ref, factor_ref, buffer_ref, sems):
    qlen = sums_ref.shape[1] // 2
    rounds = trips(table_ref)

    def into(t):
        return pltpu.make_async_copy(weight_ref.at[pl.ds(t * UNROLL, UNROLL)], buffer_ref.at[t % 2], sems.at[t % 2])

    @pl.when(rounds >= 1)
    def _():
        into(0).start()

    sums_ref[...] = jnp.zeros(sums_ref.shape, f32)
    slot = slot_ref[...]
    for k in range(SLOTS):
        for side, values in enumerate((student_ref[...], mass_ref[...])):
            part = jnp.sum(jnp.where(slot == float(k), values, 0.0), axis=1, keepdims=True)
            factor_ref[side * SLOTS + k] = jnp.broadcast_to(part, slot.shape)

    def some(t, carry):
        @pl.when(t + 1 < rounds)
        def _():
            into(t + 1).start()

        into(t).wait()
        for j in range(UNROLL):
            u = t * UNROLL + j
            grads = lax.dot_general(
                buffer_ref[t % 2, j], passage_ref[table_ref[SLOTS, u]], (((0,), (0,)), ((), ())), preferred_element_type=f32
            )
            queries = [table_ref[k, u] for k in range(SLOTS)]
            olds = [sums_ref[q] for q in queries]
            for k, q in enumerate(queries):
                part = grads[k * qlen : (k + 1) * qlen]
                student, share = factor_ref[k, pl.ds(u, 1), :], factor_ref[SLOTS + k, pl.ds(u, 1), :]
                sums_ref[q] = olds[k] + jnp.concatenate([student * part, share * part], axis=0)
        return carry

    lax.fori_loop(0, rounds, some, 0)


def join(parts_ref, local_ref, entropy_ref, sums_ref, grads_ref, loss_ref):
    group, qlen = grads_ref.shape[0], grads_ref.shape[1]
    parts = parts_ref[...]
    lane = iota((1, LANES), 1)
    total, cross, kept = (pltpu.roll(parts, LANES - (k + 1) * group, 1) for k in range(3))
    top = jnp.max(parts, axis=0, keepdims=True)
    lse = top + jnp.log(jnp.sum(total * jnp.exp(parts - top), axis=0, keepdims=True))
    agreed = jnp.sum(cross + kept * (parts - lse), axis=0, keepdims=True)
    agreed = jnp.sum(jnp.where(lane < group, agreed, 0.0), axis=1, keepdims=True)
    loss_ref[...] = jnp.broadcast_to(entropy_ref[...] - agreed, loss_ref.shape)
    factor = jnp.where(lane < group, jnp.exp(local_ref[0:1, :] - lse), 0.0)
    factors = jnp.transpose(jnp.broadcast_to(factor, (LANES, LANES)))
    for q in range(group):
        grads_ref[q] = sums_ref[q, :qlen] * factors[q : q + 1, :] - sums_ref[q, qlen:]


def body(query_tokens, passage_tokens, passage_lengths, cand_shard, cand_local, teacher_scores):
    shards, groups = lax.axis_size("passage"), lax.axis_size("query")
    me = lax.axis_index("passage")
    group, cands = cand_local.shape
    qlen, dim = query_tokens.shape[1:]
    passages, plen, _ = passage_tokens.shape
    units = 176
    padded = 256
    queries = lax.all_to_all(jnp.broadcast_to(query_tokens, (shards, qlen, dim)), "passage", 0, 0, tiled=True)
    lengths = lax.dynamic_slice_in_dim(passage_lengths, me * passages, passages).reshape(1, passages)
    table, slot, count, mass, entropy = call(
        plan,
        (
            held((16, padded), i32),
            held((units, LANES), f32),
            held((units, LANES), f32),
            held((units, LANES), f32),
            held((1, LANES), f32),
        ),
        [SMEM, VMEM, VMEM, VMEM, VMEM],
        int(2e9),
    )(me.reshape(1), cand_shard.reshape(group, cands), cand_local, teacher_scores, lengths)
    weights, student, local = call(
        score,
        (
            pltpu.HBM((units, plen, SLOTS * qlen), bf16),
            held((units, LANES), f32),
            held((8, LANES), f32),
        ),
        [SMEM, VMEM, VMEM, VMEM, VMEM, VMEM],
        int(4e9),
        [
            pltpu.VMEM(queries.shape, bf16),
            pltpu.VMEM((units, LANES), f32),
            pltpu.VMEM((2, UNROLL, plen, SLOTS * qlen), bf16),
            pltpu.SemaphoreType.DMA((2,)),
        ],
    )(table, queries, passage_tokens, slot, count, mass)
    parts = lax.all_to_all(jnp.broadcast_to(local[None, 0:1], (shards, 1, LANES)), "passage", 0, 0, tiled=True)
    (sums,) = call(
        terms_of,
        (held((group + 1, 2 * qlen, dim), f32),),
        [SMEM, HBM, VMEM, VMEM, VMEM, VMEM],
        int(4e9),
        [
            pltpu.VMEM((2 * SLOTS, units, LANES), f32),
            pltpu.VMEM((2, UNROLL, plen, SLOTS * qlen), bf16),
            pltpu.SemaphoreType.DMA((2,)),
        ],
    )(table, weights, passage_tokens, slot, student, mass)
    grads, loss = call(
        join,
        (jax.ShapeDtypeStruct((group, qlen, dim), f32), jax.ShapeDtypeStruct((1, LANES), f32)),
        [VMEM, VMEM, VMEM, VMEM],
        int(1e9),
    )(parts.reshape(shards, LANES), local, entropy, sums)
    sent = lax.all_to_all(grads, "passage", 0, 0, tiled=True)
    side = 4
    near = [[side * a + b for b in range(side)] for a in range(groups // side)]
    far = [[side * a + b for a in range(groups // side)] for b in range(side)]
    loss = lax.psum(lax.psum(loss, "query", axis_index_groups=near), "query", axis_index_groups=far)
    query_grads = jnp.sum(sent, axis=0, keepdims=True)
    return (loss[0, 0] / (groups * group), query_grads)


def solution(mesh):
    placed = (
        P(("query", "passage"), None, None),
        P("passage", None, None),
        P(),
        P("query", None, None),
        P("query", None),
        P("query", None),
    )
    return jax.shard_map(
        body,
        mesh=mesh,
        in_specs=placed,
        out_specs=(P(), P(("query", "passage"), None, None)),
        check_vma=False,
    )
```

time: 110 us -> 105 us (0.955)
  the two profiles are of different devices: /device:TPU:1 before, /device:TPU:2 now
where the time goes in v2:
time: 105 us; the launch traced here: 104 us
  Pallas kernels  36.8 us (35%)
  starting transfers between devices  23.5 us (22%)
  blocking collectives  23.5 us (22%)
  local copies, waits for them, and re-layouts  10.4 us (10%)
  waiting for transfers between devices  7.39 us (7%)
  between operations  1.92 us (2%)
    pallas_call x1, Pallas kernels, body(): call(score, (pltpu.HBM((units, plen, SLOTS * qlen), bf16), held((units, L...  18.2 us
    psum x1, blocking collectives, body(): lax.psum(lax.psum(loss, 'query', axis_index_groups=near), 'query', axis_i...  17.4 us
    pallas_call x1, Pallas kernels, body(): call(terms_of, (held((group + 1, 2 * qlen, dim), f32),), [SMEM, HBM, VMEM...  16.1 us
    all_to_all x1, starting transfers between devices, body(): lax.all_to_all(jnp.broadcast_to(query_tokens, (shards, qlen, dim)), 'pass...  10.2 us
    unnamed x23, local copies, waits for them, and re-layouts  8.22 us
    all_to_all x1, starting transfers between devices, body(): sent = lax.all_to_all(grads, 'passage', 0, 0, tiled=True)  8.03 us
    all_to_all x1, waiting for transfers between devices, body(): lax.all_to_all(jnp.broadcast_to(query_tokens, (shards, qlen, dim)), 'pass...  7.38 us
    psum x1, blocking collectives, body(): lax.psum(loss, 'query', axis_index_groups=near)  6.13 us
  transfers between devices with their start and end apart: 3, of which 1 were waited for; matrix products, arithmetic and copies ran while one was open for 1% of the time, Pallas kernels for 17%

profile of v2, /device:TPU:2, one launch (start us, length us, event | category | flops | bytes accessed | tf_op | source)
XLA Modules:
  0.0 104.1 jit_solution(18201108781238128632)
XLA Ops:
  0.6 0.0 copy-start
  0.6 1.4 %broadcast_in_dim.19 = bf16[32,32,128]{2,1,0:T(8,128)(2,1)} broadcast(bf16[32,128]{1,0:T(8,128)(2,1)} %bitcast.16), dimensions={1,2} | broadcast | bytes 270336 | tf_op jit(solution)/shard_map/broadcast_in_dim | solution.py:226
  2.1 10.2 %all-to-all-start = ((bf16[32,32,128]{2,1,0:T(8,128)(2,1)}), bf16[32,32,128]{2,1,0:T(8,128)(2,1)S(1)}, u32[]{:S(2)}, u32[]{:S(2)}) async-start(bf16[32,32,128]{2,1,0:T(8,128)(2,1)} %broadcast_in_dim.19), calls=%async_computation | async-start | bytes 524288 | tf_op jit(solution)/shard_map/all_to_all | solution.py:226
  12.3 0.8 copy.10
  13.1 0.0 copy-done
  13.1 0.1 dynamic-slice_bitcast_fusion.lengths_ref
  13.2 0.0 copy-start.2
  13.2 0.8 copy-done.2
  13.9 0.0 copy-start.3
  14.0 0.8 copy-done.3
  14.7 0.0 copy-start.1
  14.7 1.5 %shard_map.77 = (s32[16,256]{1,0:T(8,128)S(1)}, f32[176,128]{1,0:T(8,128)S(1)}, f32[176,128]{1,0:T(8,128)S(1)}, f32[176,128]{1,0:T(8,128)S(1)}, f32[1,128]{1,0:T(1,128)S(1)}) custom-call(s32[1]{0:T(128)} %bitcast.me_ref, s32[32,256]{1,0:T(8,128)S(1)} %bitcast.13, s32[32,256]{1,0:T(8,128)S(1)} %copy-done.2, f32[32,256]{1,0:T(8,128)S(1)} %copy-done.3, ...), custom_call_target="tpu_custom_call" | custom-call | flops 2000000000 | bytes 20000000 | tf_op jit(solution)/shard_map/pallas_call | solution.py:228
  16.2 0.0 copy-start.5
  16.2 0.0 copy-start.7
  16.2 7.4 %all-to-all-done.query_ref = bf16[32,32,128]{2,1,0:T(8,128)(2,1)S(1)} async-done(((bf16[32,32,128]{2,1,0:T(8,128)(2,1)}), bf16[32,32,128]{2,1,0:T(8,128)(2,1)S(1)}, u32[]{:S(2)}, u32[]{:S(2)}) %all-to-all-start) | async-done | bytes 262176 | tf_op jit(solution)/shard_map/all_to_all | solution.py:226
  23.6 0.0 copy-done.1
  23.6 18.2 %shard_map.78 = (bf16[176,128,128]{2,1,0:T(8,128)(2,1)}, f32[176,128]{1,0:T(8,128)S(1)}, f32[8,128]{1,0:T(8,128)S(1)}) custom-call(s32[16,256]{1,0:T(8,128)S(1)} %get-tuple-element.12.table_ref, bf16[32,32,128]{2,1,0:T(8,128)(2,1)S(1)} %all-to-all-done.query_ref, bf16[64,128,128]{2,1,0:T(8,128)(2,1)S(1)} %copy-done.1, ...), custom_call_target="tpu_custom_call" | custom-call | flops 4000000000 | bytes 40000000 | tf_op jit(solution)/shard_map/pallas_call | solution.py:240
  41.7 0.0 copy-done.5
  41.7 0.0 copy-done.7
  41.8 0.0 copy-start.9
  41.8 0.6 copy-done.9
  42.4 0.6 broadcast_in_dim.21
  43.0 5.3 %all-to-all-start.1 = ((f32[32,1,128]{2,1,0:T(1,128)}), f32[32,1,128]{2,1,0:T(1,128)S(1)}, u32[]{:S(2)}, u32[]{:S(2)}) async-start(f32[32,1,128]{2,1,0:T(1,128)} %broadcast_in_dim.21), calls=%async_computation.1 | async-start | bytes 32768 | tf_op jit(solution)/shard_map/all_to_all | solution.py:256
  48.3 0.0 copy-start.4
  48.3 2.6 %copy-done.4 = bf16[176,128,128]{2,1,0:T(8,128)(2,1)S(1)} copy-done((bf16[176,128,128]{2,1,0:T(8,128)(2,1)S(1)}, bf16[176,128,128]{2,1,0:T(8,128)(2,1)}, u32[]{:S(2)}) %copy-start.4) | copy-done | bytes 5767192
  50.9 0.0 copy-start.6
  50.9 0.9 copy-done.6
  51.8 0.0 copy-start.8
  51.8 0.9 copy-done.8
  52.7 0.0 copy-start.10
  52.7 0.9 copy-done.10
  53.6 16.1 %shard_map.79.sums_ref = f32[33,64,128]{2,1,0:T(8,128)S(1)} custom-call(s32[16,256]{1,0:T(8,128)S(1)} %get-tuple-element.12.table_ref, bf16[176,128,128]{2,1,0:T(8,128)(2,1)S(1)} %copy-done.4, bf16[64,128,128]{2,1,0:T(8,128)(2,1)S(1)} %copy-done.1, f32[176,128]{1,0:T(8,128)S(1)} %copy-done.6, f32[176,128]{1,0:T(8,128)S(1)} %copy-done.10, ...), custom_call_target="tpu_custom_call" | custom-call | flops 4000000000 | bytes 40000000 | tf_op jit(solution)/shard_map/pallas_call | solution.py:257
  69.7 0.0 all-to-all-done.1
  69.7 1.0 shard_map.80
  70.7 8.0 %all-to-all-start.2 = ((f32[32,32,128]{2,1,0:T(8,128)}), f32[32,32,128]{2,1,0:T(8,128)S(1)}, u32[]{:S(2)}, u32[]{:S(2)}) async-start(f32[32,32,128]{2,1,0:T(8,128)} %get-tuple-element.21), calls=%async_computation.2 | async-start | bytes 1048576 | tf_op jit(solution)/shard_map/all_to_all | solution.py:274
  78.8 6.1 %psum.14 = f32[1,128]{1,0:T(1,128)S(1)} all-reduce(f32[1,128]{1,0:T(1,128)S(1)} %get-tuple-element.20), channel_id=1, replica_groups={{0,32,64,96},{128,160,192,224},{256,288,320,352},{384,416,448,480},{1,3..., use_global_device_ids=true, to_apply=%region_0.0 | all-reduce | flops 128 | bytes 1024 | tf_op jit(solution)/shard_map/psum | solution.py:278
  84.9 17.4 %psum.15 = f32[1,128]{1,0:T(1,128)S(1)} all-reduce(f32[1,128]{1,0:T(1,128)S(1)} %psum.14), channel_id=1, replica_groups={{0,128,256,384},{32,160,288,416},{64,192,320,448},{96,224,352,480},{1,1..., use_global_device_ids=true, to_apply=%region_1.0 | all-reduce | flops 128 | bytes 1024 | tf_op jit(solution)/shard_map/psum | solution.py:278
  102.3 0.0 all-to-all-done.2
  102.4 0.7 reduce_sum.9
  (1 shorter events, 0.0 us)
Async XLA Ops:
  0.6 12.5 %copy-start = (s32[2048]{0:T(1024)S(1)}, s32[2048]{0:T(1024)}, u32[]{:S(2)}) copy-start(s32[2048]{0:T(1024)} %param.8) | copy-start | bytes 24580
  2.1 21.5 %all-to-all-start = ((bf16[32,32,128]{2,1,0:T(8,128)(2,1)}), bf16[32,32,128]{2,1,0:T(8,128)(2,1)S(1)}, u32[]{:S(2)}, u32[]{:S(2)}) async-start(bf16[32,32,128]{2,1,0:T(8,128)(2,1)} %broadcast_in_dim.19), calls=%async_computation | async-start | bytes 524288 | tf_op jit(solution)/shard_map/all_to_all | solution.py:226
  13.2 0.8 copy-start.2
  13.9 0.8 copy-start.3
  14.7 8.9 %copy-start.1 = (bf16[64,128,128]{2,1,0:T(8,128)(2,1)S(1)}, bf16[64,128,128]{2,1,0:T(8,128)(2,1)}, u32[]{:S(2)}) copy-start(bf16[64,128,128]{2,1,0:T(8,128)(2,1)} %passage_ref.3) | copy-start | bytes 6291460
  16.2 25.6 %copy-start.5 = (f32[176,128]{1,0:T(8,128)}, f32[176,128]{1,0:T(8,128)S(1)}, u32[]{:S(2)}) copy-start(f32[176,128]{1,0:T(8,128)S(1)} %get-tuple-element.13.slot_ref) | copy-start | bytes 270340
  16.2 25.6 %copy-start.7 = (f32[176,128]{1,0:T(8,128)}, f32[176,128]{1,0:T(8,128)S(1)}, u32[]{:S(2)}) copy-start(f32[176,128]{1,0:T(8,128)S(1)} %get-tuple-element.15.mass_ref) | copy-start | bytes 270340
  41.8 0.6 copy-start.9
  43.0 26.7 %all-to-all-start.1 = ((f32[32,1,128]{2,1,0:T(1,128)}), f32[32,1,128]{2,1,0:T(1,128)S(1)}, u32[]{:S(2)}, u32[]{:S(2)}) async-start(f32[32,1,128]{2,1,0:T(1,128)} %broadcast_in_dim.21), calls=%async_computation.1 | async-start | bytes 32768 | tf_op jit(solution)/shard_map/all_to_all | solution.py:256
  48.3 2.6 %copy-start.4 = (bf16[176,128,128]{2,1,0:T(8,128)(2,1)S(1)}, bf16[176,128,128]{2,1,0:T(8,128)(2,1)}, u32[]{:S(2)}) copy-start(bf16[176,128,128]{2,1,0:T(8,128)(2,1)} %get-tuple-element.18.weight_ref) | copy-start | bytes 17301508
  50.9 0.9 copy-start.6
  51.8 0.9 copy-start.8
  52.7 0.9 copy-start.10
  70.7 31.6 %all-to-all-start.2 = ((f32[32,32,128]{2,1,0:T(8,128)}), f32[32,32,128]{2,1,0:T(8,128)S(1)}, u32[]{:S(2)}, u32[]{:S(2)}) async-start(f32[32,32,128]{2,1,0:T(8,128)} %get-tuple-element.21), calls=%async_computation.2 | async-start | bytes 1048576 | tf_op jit(solution)/shard_map/all_to_all | solution.py:274

commit v3 on v2

v3 whole, which is shorter than its diff:
```python
import math
import jax
import jax.numpy as jnp
from jax import lax
from jax.experimental import pallas as pl
from jax.experimental.pallas import tpu as pltpu
from jax.sharding import PartitionSpec as P

LANES = 128
SLOTS = 4
UNROLL = 8
UNITS = 176
PLEN = 128
PADDED = 256
PAIR = 2
FLOOR = -1e30
NT = (((1,), (1,)), ((), ()))
VMEM = pl.BlockSpec(memory_space=pltpu.VMEM)
HBM = pl.BlockSpec(memory_space=pltpu.HBM)
SMEM = pl.BlockSpec(memory_space=pltpu.SMEM)
f32 = jnp.float32
bf16 = jnp.bfloat16
i32 = jnp.int32


def held(shape, dtype):
    return pltpu.VMEM(shape, dtype)


def in_hbm(array):
    return pltpu.with_memory_space_constraint(array, pltpu.HBM)


def call(kernel, outs, in_specs, cost, scratch=()):
    return pl.pallas_call(
        kernel,
        out_shape=outs,
        in_specs=in_specs,
        out_specs=tuple(HBM if getattr(o, "memory_space", None) == pltpu.HBM else VMEM for o in outs),
        scratch_shapes=scratch,
        compiler_params=pltpu.CompilerParams(vmem_limit_bytes=24 * 1024 * 1024),
        cost_estimate=pl.CostEstimate(flops=cost, bytes_accessed=cost // 100, transcendentals=0),
    )


def iota(shape, axis):
    return lax.broadcasted_iota(i32, shape, axis)


def plan(me_ref, shard_ref, local_ref, teacher_ref, lengths_ref, table_ref, slot_ref, count_ref, mass_ref, share_ref, entropy_ref):
    group, passages = shard_ref.shape[0], lengths_ref.shape[1]
    units, padded = count_ref.shape[0], PADDED
    teacher = teacher_ref[...]
    top = jnp.max(teacher, axis=1, keepdims=True)
    log_teacher = teacher - (top + jnp.log(jnp.sum(jnp.exp(teacher - top), axis=1, keepdims=True)))
    probs = jnp.exp(log_teacher)
    here = shard_ref[...] == me_ref[0]
    entropy_ref[...] = jnp.broadcast_to(jnp.sum(jnp.where(here, probs * log_teacher, 0.0), keepdims=True), entropy_ref.shape)
    key = jnp.where(here, local_ref[...], -1)
    row = iota((passages, key.shape[1]), 0)
    lane = iota((passages, LANES), 1)
    count = jnp.zeros((passages, LANES), f32)
    mass = jnp.zeros((passages, LANES), f32)
    for q in range(group):
        hit = key[q : q + 1, :] == row
        count = jnp.where(lane == q, jnp.sum(jnp.where(hit, 1.0, 0.0), axis=1, keepdims=True), count)
        mass = jnp.where(lane == q, jnp.sum(jnp.where(hit, probs[q : q + 1, :], 0.0), axis=1, keepdims=True), mass)
    live = count > 0.0
    live_b = jnp.where(live, 1.0, 0.0).astype(bf16)
    before = jnp.where(iota((LANES, LANES), 0) < iota((LANES, LANES), 1), 1.0, 0.0).astype(bf16)
    rank = jnp.dot(live_b, before, preferred_element_type=f32)
    rank = jnp.where(live, rank, -1.0)
    named = lax.dot_general(jnp.ones((8, LANES), bf16), live_b, NT, preferred_element_type=f32)
    needed = ((named.astype(i32) + (SLOTS - 1)) // SLOTS).astype(f32)
    before_p = jnp.where(iota((passages, passages), 0) < iota((passages, passages), 1), 1.0, 0.0).astype(bf16)
    first = jnp.dot(needed.astype(bf16), before_p, preferred_element_type=f32)
    needed, first = needed[0:1, :], first[0:1, :]
    total = jnp.sum(needed, axis=1, keepdims=True)
    unit = iota((padded, passages), 0).astype(f32)
    own = (unit >= first) & (unit < first + needed)
    own_f = jnp.where(own, 1.0, 0.0)
    own_b = own_f.astype(bf16)
    passage = jnp.sum(jnp.where(own, iota((padded, passages), 1).astype(f32), 0.0), axis=1, keepdims=True)
    length = jnp.sum(jnp.where(own, lengths_ref[...].astype(f32), 0.0), axis=1, keepdims=True)
    offset = jnp.sum(jnp.where(own, unit - first, 0.0), axis=1, keepdims=True) * SLOTS
    wide = iota((padded, LANES), 1)
    used = iota((padded, LANES), 0).astype(f32) < total
    unit_rank = jnp.dot(own_b, rank.astype(bf16), preferred_element_type=f32)
    slot = jnp.where(used & (unit_rank >= 0.0), unit_rank - offset, -1.0)
    here = (slot >= 0.0) & (slot < float(SLOTS))
    slot = jnp.where(here, slot, -1.0)
    unit_count = jnp.where(here, jnp.dot(own_b, count.astype(bf16), preferred_element_type=f32), 0.0)
    unit_mass = jnp.dot(own_f, mass, preferred_element_type=f32, precision=lax.Precision.HIGHEST)
    unit_mass = jnp.where(here, unit_mass, 0.0)
    slot_ref[...] = slot[:units]
    count_ref[...] = unit_count[:units]
    mass_ref[...] = unit_mass[:units]
    ints = jnp.where(wide == SLOTS, passage, 0.0)
    eights = jnp.floor(length * 0.125) * 8.0
    ints = jnp.where(wide == SLOTS + 1, PLEN - eights, ints)
    ints = jnp.where(wide == SLOTS + 3, length - eights, ints)
    ints = jnp.where(wide == SLOTS + 2, total, ints)
    wide_f = wide.astype(f32)
    shares = jnp.zeros((units, LANES), f32)
    for k in range(SLOTS):
        pick = slot == float(k)
        query = group + jnp.sum(jnp.where(pick, wide_f - group, 0.0), axis=1, keepdims=True)
        ints = jnp.where(wide == k, query, ints)
        share = jnp.sum(jnp.where(pick, unit_mass, 0.0)[:units], axis=1, keepdims=True)
        shares = jnp.where(wide[:units] == SLOTS + k, share, shares)
    share_ref[...] = shares
    ints = jnp.transpose(ints).astype(i32)
    for k in range(SLOTS + 4):
        for half in range(padded // LANES):
            table_ref[pl.ds(k * (padded // LANES) + half, 1), :] = ints[k : k + 1, half * LANES : (half + 1) * LANES]


def field(k):
    return k * PADDED


def trips(table_ref):
    return (table_ref[field(SLOTS + 2)] + (UNROLL - 1)) // UNROLL


def score(
    table_ref, query_ref, passage_ref, slot_ref, count_ref, mass_ref, share_ref, entropy_ref,
    weight_ref, factor_ref, local_ref,
    double_ref, row_ref, logits_ref, buffer_ref, scale_ref, cap_ref, sems,
):
    group, qlen = query_ref.shape[0], query_ref.shape[1]
    units, columns, plen = weight_ref.shape
    double_ref[:group] = query_ref[...] * 2
    double_ref[group] = jnp.zeros(double_ref.shape[1:], bf16)
    row_ref[...] = jnp.zeros(row_ref.shape, f32)
    logits_ref[...] = jnp.zeros(logits_ref.shape, f32)
    for part in range(8):
        cap_ref[part] = jnp.where(iota((2 * plen, columns), 0) < plen + part, -FLOOR, FLOOR)
    rounds = trips(table_ref)

    def out(t):
        first = pl.multiple_of(t * UNROLL, UNROLL)
        return pltpu.make_async_copy(
            buffer_ref.at[pl.ds(first + UNROLL, UNROLL)], weight_ref.at[pl.ds(first, UNROLL)], sems.at[t]
        )

    def some(t, carry):
        for j in range(UNROLL):
            u = t * UNROLL + j
            old = logits_ref[j]
            p = table_ref[field(SLOTS) + u]
            tokens = jnp.concatenate([double_ref[table_ref[field(k) + u]] for k in range(SLOTS)], axis=0)
            logits = lax.dot_general(passage_ref[p], tokens, NT, preferred_element_type=f32)
            start = pl.multiple_of(table_ref[field(SLOTS + 1) + u], 8)
            logits_ref[j] = jnp.minimum(logits, cap_ref[table_ref[field(SLOTS + 3) + u], pl.ds(start, plen), :])
            top = jnp.max(old, axis=0, keepdims=True)
            terms = jnp.exp(old - top)
            total = jnp.sum(terms, axis=0, keepdims=True)
            buffer_ref[u] = jnp.transpose((terms * (1.0 / total)).astype(bf16))
            row_ref[pl.ds(u, 1), :] = top + jnp.log(total)

        @pl.when(t > 0)
        def _():
            out(t - 1).start()

        return carry

    lax.fori_loop(0, rounds + 1, some, 0)
    same = iota((columns, LANES), 0) // qlen == iota((columns, LANES), 1)
    rows = row_ref[pl.ds(UNROLL, units), :]
    summed = jnp.dot(rows, jnp.where(same, 0.5, 0.0), preferred_element_type=f32, precision=lax.Precision.HIGHEST)
    slot, count, mass = slot_ref[...], count_ref[...], mass_ref[...]
    scores = jnp.zeros((units, LANES), f32)
    for k in range(SLOTS):
        scores = jnp.where(slot == float(k), jnp.broadcast_to(summed[:, k : k + 1], (units, LANES)), scores)
    live = slot >= 0.0
    top = jnp.max(jnp.where(live, scores, FLOOR), axis=0, keepdims=True)
    gap = jnp.where(live, scores - top, 0.0)
    student = jnp.where(live, count * jnp.exp(gap), 0.0)
    scale = share_ref[...]
    wide = iota((units, LANES), 1)
    for k in range(SLOTS):
        scale = jnp.where(wide == k, jnp.sum(jnp.where(slot == float(k), student, 0.0), axis=1, keepdims=True), scale)
    scale_ref[...] = scale
    factors = pltpu.make_async_copy(scale_ref, factor_ref, sems.at[units // UNROLL])
    factors.start()
    total = jnp.sum(student, axis=0, keepdims=True)
    lane = iota((1, LANES), 1)
    cross = jnp.sum(mass * gap, axis=0, keepdims=True) - jnp.where(lane == 0, entropy_ref[...], 0.0)
    kept = jnp.sum(mass, axis=0, keepdims=True)
    packed = jnp.where(lane < group, top, 0.0)
    for k, part in enumerate((total, cross, kept)):
        moved = pltpu.roll(jnp.broadcast_to(part, (8, LANES)), (k + 1) * group, 1)[0:1]
        packed = jnp.where(lane // group == k + 1, moved, packed)
    local_ref[...] = jnp.broadcast_to(packed, local_ref.shape)

    def finish(t, carry):
        out(t).wait()
        return carry

    lax.fori_loop(0, rounds, finish, 0)
    factors.wait()


def terms_of(table_ref, weight_ref, passage_ref, factor_ref, sums_ref, scale_ref, spread_ref, grads_ref, buffer_ref, sems):
    qlen = sums_ref.shape[1] // 2
    units = weight_ref.shape[0]
    rounds = trips(table_ref)
    factors = pltpu.make_async_copy(factor_ref, scale_ref, sems.at[units // UNROLL])
    factors.start()

    def into(t):
        part = pl.ds(pl.multiple_of(t * UNROLL, UNROLL), UNROLL)
        return pltpu.make_async_copy(weight_ref.at[part], buffer_ref.at[part], sems.at[t])

    def begin(t, carry):
        into(t).start()
        return carry

    lax.fori_loop(0, rounds, begin, 0)
    sums_ref[...] = jnp.zeros(sums_ref.shape, f32)
    grads_ref[...] = jnp.zeros(grads_ref.shape, f32)
    factors.wait()
    scale = scale_ref[...]
    for k in range(2 * SLOTS):
        spread_ref[k] = jnp.broadcast_to(scale[:, k : k + 1], scale.shape)

    def some(t, carry):
        @pl.when(t < rounds)
        def _():
            into(t).wait()

        for j in range(UNROLL):
            old = grads_ref[j]
            late = jnp.minimum(t, rounds - 1) * UNROLL + j
            grads_ref[j] = jnp.dot(buffer_ref[late], passage_ref[table_ref[field(SLOTS) + late]], preferred_element_type=f32)
            u = jnp.maximum(t - 1, 0) * UNROLL + j
            queries = [table_ref[field(k) + u] for k in range(SLOTS)]
            sums = [sums_ref[q] for q in queries]
            for k, q in enumerate(queries):
                part = old[k * qlen : (k + 1) * qlen]
                student, share = spread_ref[k, pl.ds(u, 1), :], spread_ref[SLOTS + k, pl.ds(u, 1), :]
                sums_ref[q] = sums[k] + jnp.concatenate([student * part, share * part], axis=0)
        return carry

    @pl.when(rounds > 0)
    def _():
        lax.fori_loop(0, rounds + 1, some, 0)


def join(side_ref, parts_ref, local_ref, sums_ref, grads_ref, loss_ref):
    group, qlen = grads_ref.shape[0], grads_ref.shape[1]
    lane = iota((1, LANES), 1)
    loss = jnp.zeros((1, 1), f32)
    lses = []
    for side in range(parts_ref.shape[0] // group):
        parts = parts_ref[side * group : (side + 1) * group]
        total, cross, kept = (pltpu.roll(parts, LANES - (k + 1) * group, 1) for k in range(3))
        top = jnp.max(parts, axis=0, keepdims=True)
        lse = top + jnp.log(jnp.sum(total * jnp.exp(parts - top), axis=0, keepdims=True))
        agreed = jnp.sum(cross + kept * (parts - lse), axis=0, keepdims=True)
        loss = loss - jnp.sum(jnp.where(lane < group, agreed, 0.0), axis=1, keepdims=True)
        lses.append(lse)
    loss_ref[...] = jnp.broadcast_to(loss, loss_ref.shape)
    lse = lses[0]
    for side in range(1, len(lses)):
        lse = jnp.where(side_ref[0] == side, lses[side], lse)
    factor = jnp.where(lane < group, jnp.exp(local_ref[0:1, :] - lse), 0.0)
    factors = jnp.transpose(jnp.broadcast_to(factor, (LANES, LANES)))
    for q in range(group):
        grads_ref[q] = sums_ref[q, :qlen] * factors[q : q + 1, :] - sums_ref[q, qlen:]


def body(query_tokens, passage_tokens, passage_lengths, cand_shard, cand_local, teacher_scores):
    shards, groups = lax.axis_size("passage"), lax.axis_size("query")
    me, own = lax.axis_index("passage"), lax.axis_index("query")
    group, cands = cand_local.shape
    qlen, dim = query_tokens.shape[1:]
    passages, plen, _ = passage_tokens.shape
    units = UNITS
    queries = lax.all_to_all(jnp.broadcast_to(query_tokens, (shards, qlen, dim)), "passage", 0, 0, tiled=True)
    lengths = lax.dynamic_slice_in_dim(passage_lengths, me * passages, passages).reshape(1, passages)
    table, slot, count, mass, share, entropy = call(
        plan,
        (
            held((2 * SLOTS * PADDED // LANES, LANES), i32),
            held((units, LANES), f32),
            held((units, LANES), f32),
            held((units, LANES), f32),
            held((units, LANES), f32),
            held((1, LANES), f32),
        ),
        [SMEM, VMEM, VMEM, VMEM, VMEM],
        int(2e9),
    )(me.reshape(1), cand_shard.reshape(group, cands), cand_local, teacher_scores, lengths)
    weights, factors, local = call(
        score,
        (
            pltpu.HBM((units, SLOTS * qlen, plen), bf16),
            pltpu.HBM((units, LANES), f32),
            held((PAIR * shards, LANES), f32),
        ),
        [SMEM, VMEM, VMEM, VMEM, VMEM, VMEM, VMEM, VMEM],
        int(4e9),
        [
            pltpu.VMEM((group + 1, qlen, dim), bf16),
            pltpu.VMEM((UNROLL + units, LANES), f32),
            pltpu.VMEM((UNROLL, plen, SLOTS * qlen), f32),
            pltpu.VMEM((UNROLL + units, SLOTS * qlen, plen), bf16),
            pltpu.VMEM((units, LANES), f32),
            pltpu.VMEM((8, 2 * plen, SLOTS * qlen), f32),
            pltpu.SemaphoreType.DMA((units // UNROLL + 1,)),
        ],
    )(table.reshape(-1), queries, passage_tokens, slot, count, mass, share, entropy)
    pairs = [[g * shards + s for g in range(a, a + PAIR) for s in range(shards)] for a in range(0, groups, PAIR)]
    parts = lax.all_to_all(
        local.reshape(PAIR * shards, 1, LANES), ("query", "passage"), 0, 0, tiled=True, axis_index_groups=pairs
    )
    (sums,) = call(
        terms_of,
        (held((group + 1, 2 * qlen, dim), f32),),
        [SMEM, HBM, VMEM, HBM],
        int(4e9),
        [
            pltpu.VMEM((units, LANES), f32),
            pltpu.VMEM((2 * SLOTS, units, LANES), f32),
            pltpu.VMEM((UNROLL, SLOTS * qlen, dim), f32),
            pltpu.VMEM((units, SLOTS * qlen, plen), bf16),
            pltpu.SemaphoreType.DMA((units // UNROLL + 1,)),
        ],
    )(table.reshape(-1), in_hbm(weights), passage_tokens, in_hbm(factors))
    grads, loss = call(
        join,
        (jax.ShapeDtypeStruct((group, qlen, dim), f32), jax.ShapeDtypeStruct((1, LANES), f32)),
        [SMEM, VMEM, VMEM, VMEM],
        int(1e9),
    )((own % PAIR).reshape(1), parts.reshape(PAIR * shards, LANES), local, sums)
    sent = lax.all_to_all(grads, "passage", 0, 0, tiled=True)
    rings = [list(range(a, groups, PAIR)) for a in range(PAIR)]
    loss = lax.psum(loss, "query", axis_index_groups=rings)
    query_grads = jnp.sum(sent, axis=0, keepdims=True)
    return (loss[0, 0] / (groups * group), query_grads)


def solution(mesh):
    placed = (
        P(("query", "passage"), None, None),
        P("passage", None, None),
        P(),
        P("query", None, None),
        P("query", None),
        P("query", None),
    )
    return jax.shard_map(
        body,
        mesh=mesh,
        in_specs=placed,
        out_specs=(P(), P(("query", "passage"), None, None)),
        check_vma=False,
    )
```

time: 105 us -> 81.5 us (0.78)
  Pallas kernels: 36.8 us -> 14.3 us
  local copies, waits for them, and re-layouts: 10.4 us -> 3.8 us
  waiting for transfers between devices: 7.39 us -> 11 us
  starting transfers between devices: 23.5 us -> 25.9 us
    pallas_call x2, Pallas kernels: 19.6 us -> 7.94 us  [the longest x1 6.38 us: body(): call(score, (pltpu.HBM((units, SLOTS * qlen, plen), bf16), pltpu.HBM((uni...]
    pallas_call x1, Pallas kernels: 16.1 us -> 4.57 us  [body(): call(terms_of, (held((group + 1, 2 * qlen, dim), f32),), [SMEM, HBM, VMEM...]
    unnamed x23 -> x9, local copies, waits for them, and re-layouts: 8.22 us -> 2.29 us
    all_to_all x1, starting transfers between devices: 5.27 us -> 9 us  [body(): lax.all_to_all(local.reshape(PAIR * shards, 1, LANES), ('query', 'passage...]
    all_to_all x1, waiting for transfers between devices: 0.01 us -> 3.7 us  [body(): lax.all_to_all(local.reshape(PAIR * shards, 1, LANES), ('query', 'passage...]
    all_to_all x1, starting transfers between devices: 8.03 us -> 6.68 us  [body(): sent = lax.all_to_all(grads, 'passage', 0, 0, tiled=True)]
    psum x2 -> x1, blocking collectives: 23.5 us -> 23.3 us  [body(): loss = lax.psum(loss, 'query', axis_index_groups=rings)]
  transfers between devices with their start and end apart: 3 -> 3, of which waited for: 1 -> 2; matrix products, arithmetic and copies ran while one was open for 1% -> 1% of each run, Pallas kernels for 17% -> 8%
where the time goes in v3:
time: 81.5 us; the launch traced here: 80.9 us
  starting transfers between devices  25.9 us (32%)
  blocking collectives  23.3 us (29%)
  Pallas kernels  14.3 us (18%)
  waiting for transfers between devices  11 us (13%)
  local copies, waits for them, and re-layouts  3.8 us (5%)
  between operations  1.88 us (2%)
    psum x1, blocking collectives, body(): loss = lax.psum(loss, 'query', axis_index_groups=rings)  23.3 us
    all_to_all x1, starting transfers between devices, body(): lax.all_to_all(jnp.broadcast_to(query_tokens, (shards, qlen, dim)), 'pass...  10.2 us
    all_to_all x1, starting transfers between devices, body(): lax.all_to_all(local.reshape(PAIR * shards, 1, LANES), ('query', 'passage...  9 us
    all_to_all x1, waiting for transfers between devices, body(): lax.all_to_all(jnp.broadcast_to(query_tokens, (shards, qlen, dim)), 'pass...  7.28 us
    all_to_all x1, starting transfers between devices, body(): sent = lax.all_to_all(grads, 'passage', 0, 0, tiled=True)  6.68 us
    pallas_call x1, Pallas kernels, body(): call(score, (pltpu.HBM((units, SLOTS * qlen, plen), bf16), pltpu.HBM((uni...  6.38 us
    pallas_call x1, Pallas kernels, body(): call(terms_of, (held((group + 1, 2 * qlen, dim), f32),), [SMEM, HBM, VMEM...  4.57 us
    all_to_all x1, waiting for transfers between devices, body(): lax.all_to_all(local.reshape(PAIR * shards, 1, LANES), ('query', 'passage...  3.7 us
  transfers between devices with their start and end apart: 3, of which 2 were waited for; matrix products, arithmetic and copies ran while one was open for 1% of the time, Pallas kernels for 8%

profile of v3, /device:TPU:2, one launch (start us, length us, event | category | flops | bytes accessed | tf_op | source)
XLA Modules:
  0.0 80.9 jit_solution(3037575213800190963)
XLA Ops:
  0.6 0.0 copy-start
  0.6 1.4 %broadcast_in_dim.11 = bf16[32,32,128]{2,1,0:T(8,128)(2,1)} broadcast(bf16[32,128]{1,0:T(8,128)(2,1)} %bitcast.21), dimensions={1,2} | broadcast | bytes 270336 | tf_op jit(solution)/shard_map/broadcast_in_dim | solution.py:281
  2.1 10.2 %all-to-all-start = ((bf16[32,32,128]{2,1,0:T(8,128)(2,1)}), bf16[32,32,128]{2,1,0:T(8,128)(2,1)S(1)}, u32[]{:S(2)}, u32[]{:S(2)}) async-start(bf16[32,32,128]{2,1,0:T(8,128)(2,1)} %broadcast_in_dim.11), calls=%async_computation | async-start | bytes 524288 | tf_op jit(solution)/shard_map/all_to_all | solution.py:281
  12.3 0.8 copy.11
  13.1 0.0 copy-done
  13.1 0.1 dynamic-slice_bitcast_fusion.lengths_ref
  13.2 0.0 copy-start.2
  13.2 0.8 copy-done.2
  13.9 0.0 copy-start.3
  13.9 0.8 copy-done.3
  14.7 0.0 copy-start.1
  14.7 1.6 %shard_map.77 = (s32[16,128]{1,0:T(8,128)S(1)}, f32[176,128]{1,0:T(8,128)S(1)}, f32[176,128]{1,0:T(8,128)S(1)}, f32[176,128]{1,0:T(8,128)S(1)}, f32[176,128]{1,0:T(8,128)S(1)}, /*index=5*/f32[1,128]{1,0:T(1,128)S(1)}) custom-call(s32[1]{0:T(128)} %bitcast.1.me_ref, s32[32,256]{1,0:T(8,128)S(1)} %bitcast.16, s32[32,256]{1,0:T(8,128)S(1)} %copy-done.2, ...), custom_call_target="tpu_custom_call" | custom-call | flops 2000000000 | bytes 20000000 | tf_op jit(solution)/shard_map/pallas_call | solution.py:283
  16.3 7.3 %all-to-all-done.query_ref = bf16[32,32,128]{2,1,0:T(8,128)(2,1)S(1)} async-done(((bf16[32,32,128]{2,1,0:T(8,128)(2,1)}), bf16[32,32,128]{2,1,0:T(8,128)(2,1)S(1)}, u32[]{:S(2)}, u32[]{:S(2)}) %all-to-all-start) | async-done | bytes 262176 | tf_op jit(solution)/shard_map/all_to_all | solution.py:281
  23.6 0.0 copy-done.1
  23.6 6.4 %shard_map.78 = (bf16[176,128,128]{2,1,0:T(8,128)(2,1)}, f32[176,128]{1,0:T(8,128)}, f32[64,128]{1,0:T(8,128)}) custom-call(s32[2048]{0:T(1024)S(1)} %bitcast.18, bf16[32,32,128]{2,1,0:T(8,128)(2,1)S(1)} %all-to-all-done.query_ref, bf16[64,128,128]{2,1,0:T(8,128)(2,1)S(1)} %copy-done.1, f32[176,128]{1,0:T(8,128)S(1)} %get-tuple-element.14.slot_ref, ...), custom_call_target="tpu_custom_call" | custom-call | flops 4000000000 | bytes 40000000 | tf_op jit(solution)/shard_map/pallas_call | solution.py:296
  29.9 9.0 %all-to-all-start.1 = ((f32[64,1,128]{2,1,0:T(1,128)}), f32[64,1,128]{2,1,0:T(1,128)S(1)}, u32[]{:S(2)}, u32[]{:S(2)}) async-start(f32[64,1,128]{2,1,0:T(1,128)} %bitcast.6), calls=%async_computation.1 | async-start | bytes 65536 | tf_op jit(solution)/shard_map/all_to_all | solution.py:316
  38.9 4.6 %shard_map.79.sums_ref = f32[33,64,128]{2,1,0:T(8,128)S(1)} custom-call(s32[2048]{0:T(1024)S(1)} %bitcast.19, bf16[176,128,128]{2,1,0:T(8,128)(2,1)} %get-tuple-element.20.weight_ref, bf16[64,128,128]{2,1,0:T(8,128)(2,1)S(1)} %copy-done.1, f32[176,128]{1,0:T(8,128)} %get-tuple-element.21.factor_ref), custom_call_target="tpu_custom_call" | custom-call | flops 4000000000 | bytes 40000000 | tf_op jit(solution)/shard_map/pallas_call | solution.py:319
  43.5 3.7 %all-to-all-done.1 = f32[64,1,128]{2,1,0:T(1,128)S(1)} async-done(((f32[64,1,128]{2,1,0:T(1,128)}), f32[64,1,128]{2,1,0:T(1,128)S(1)}, u32[]{:S(2)}, u32[]{:S(2)}) %all-to-all-start.1) | async-done | bytes 32800 | tf_op jit(solution)/shard_map/all_to_all | solution.py:316
  47.2 1.8 %shard_map.80 = (f32[32,32,128]{2,1,0:T(8,128)}, f32[1,128]{1,0:T(1,128)S(1)}) custom-call(s32[1]{0:T(128)} %bitcast.side_ref, f32[64,128]{1,0:T(8,128)S(1)} %bitcast.17, f32[64,128]{1,0:T(8,128)} %get-tuple-element.19.local_ref, f32[33,64,128]{2,1,0:T(8,128)S(1)} %shard_map.79.sums_ref), custom_call_target="tpu_custom_call" | custom-call | flops 1000000000 | bytes 10000000 | tf_op jit(solution)/shard_map/pallas_call | solution.py:332
  49.0 6.7 %all-to-all-start.2 = ((f32[32,32,128]{2,1,0:T(8,128)}), f32[32,32,128]{2,1,0:T(8,128)S(1)}, u32[]{:S(2)}, u32[]{:S(2)}) async-start(f32[32,32,128]{2,1,0:T(8,128)} %get-tuple-element.23), calls=%async_computation.2 | async-start | bytes 1048576 | tf_op jit(solution)/shard_map/all_to_all | solution.py:338
  55.7 23.3 %psum.7 = f32[1,128]{1,0:T(1,128)S(1)} all-reduce(f32[1,128]{1,0:T(1,128)S(1)} %get-tuple-element.22), channel_id=1, replica_groups={{0,64,128,192,256,320,384,448},{32,96,160,224,288,352,416,480},{1,65,12..., use_global_device_ids=true, to_apply=%region_0.1 | all-reduce | flops 128 | bytes 1024 | tf_op jit(solution)/shard_map/psum | solution.py:340
  79.1 0.0 all-to-all-done.2
  79.1 0.7 reduce_sum.9
Async XLA Ops:
  0.6 12.5 %copy-start = (s32[2048]{0:T(1024)S(1)}, s32[2048]{0:T(1024)}, u32[]{:S(2)}) copy-start(s32[2048]{0:T(1024)} %param.8) | copy-start | bytes 24580
  2.1 21.5 %all-to-all-start = ((bf16[32,32,128]{2,1,0:T(8,128)(2,1)}), bf16[32,32,128]{2,1,0:T(8,128)(2,1)S(1)}, u32[]{:S(2)}, u32[]{:S(2)}) async-start(bf16[32,32,128]{2,1,0:T(8,128)(2,1)} %broadcast_in_dim.11), calls=%async_computation | async-start | bytes 524288 | tf_op jit(solution)/shard_map/all_to_all | solution.py:281
  13.2 0.8 copy-start.2
  13.9 0.8 copy-start.3
  14.7 8.8 %copy-start.1 = (bf16[64,128,128]{2,1,0:T(8,128)(2,1)S(1)}, bf16[64,128,128]{2,1,0:T(8,128)(2,1)}, u32[]{:S(2)}) copy-start(bf16[64,128,128]{2,1,0:T(8,128)(2,1)} %passage_ref.3) | copy-start | bytes 6291460
  29.9 17.3 %all-to-all-start.1 = ((f32[64,1,128]{2,1,0:T(1,128)}), f32[64,1,128]{2,1,0:T(1,128)S(1)}, u32[]{:S(2)}, u32[]{:S(2)}) async-start(f32[64,1,128]{2,1,0:T(1,128)} %bitcast.6), calls=%async_computation.1 | async-start | bytes 65536 | tf_op jit(solution)/shard_map/all_to_all | solution.py:316
  49.0 30.1 %all-to-all-start.2 = ((f32[32,32,128]{2,1,0:T(8,128)}), f32[32,32,128]{2,1,0:T(8,128)S(1)}, u32[]{:S(2)}, u32[]{:S(2)}) async-start(f32[32,32,128]{2,1,0:T(8,128)} %get-tuple-element.23), calls=%async_computation.2 | async-start | bytes 1048576 | tf_op jit(solution)/shard_map/all_to_all | solution.py:338

commit v4 on v3

--- a/solution.py
+++ b/solution.py
@@ -12,7 +12,7 @@
 UNITS = 176
 PLEN = 128
 PADDED = 256
-PAIR = 2
+TOLD = 4
 FLOOR = -1e30
 NT = (((1,), (1,)), ((), ()))
 VMEM = pl.BlockSpec(memory_space=pltpu.VMEM)
@@ -47,14 +47,14 @@
     return lax.broadcasted_iota(i32, shape, axis)
 
 
-def plan(me_ref, shard_ref, local_ref, teacher_ref, lengths_ref, table_ref, slot_ref, count_ref, mass_ref, share_ref, entropy_ref):
+def plan(shard_ref, local_ref, teacher_ref, lengths_ref, table_ref, slot_ref, count_ref, mass_ref, share_ref, entropy_ref):
     group, passages = shard_ref.shape[0], lengths_ref.shape[1]
     units, padded = count_ref.shape[0], PADDED
     teacher = teacher_ref[...]
     top = jnp.max(teacher, axis=1, keepdims=True)
     log_teacher = teacher - (top + jnp.log(jnp.sum(jnp.exp(teacher - top), axis=1, keepdims=True)))
     probs = jnp.exp(log_teacher)
-    here = shard_ref[...] == me_ref[0]
+    here = shard_ref[...] == lax.axis_index("passage")
     entropy_ref[...] = jnp.broadcast_to(jnp.sum(jnp.where(here, probs * log_teacher, 0.0), keepdims=True), entropy_ref.shape)
     key = jnp.where(here, local_ref[...], -1)
     row = iota((passages, key.shape[1]), 0)
@@ -248,24 +248,32 @@
         lax.fori_loop(0, rounds + 1, some, 0)
 
 
-def join(side_ref, parts_ref, local_ref, sums_ref, grads_ref, loss_ref):
+def shared(parts):
+    group = LANES // 4
+    total, cross, kept = (pltpu.roll(parts, LANES - (k + 1) * group, 1) for k in range(3))
+    top = jnp.max(parts, axis=0, keepdims=True)
+    lse = top + jnp.log(jnp.sum(total * jnp.exp(parts - top), axis=0, keepdims=True))
+    return lse, cross, kept
+
+
+def losses(parts_ref, loss_ref):
+    shards = parts_ref.shape[0] // TOLD
+    loss = jnp.zeros((1, 1), f32)
+    for side in range(TOLD):
+        parts = parts_ref[side * shards : (side + 1) * shards]
+        lse, cross, kept = shared(parts)
+        agreed = jnp.sum(cross + kept * (parts - lse), axis=0, keepdims=True)
+        loss = loss - jnp.sum(jnp.where(iota((1, LANES), 1) < LANES // 4, agreed, 0.0), axis=1, keepdims=True)
+    loss_ref[...] = jnp.broadcast_to(loss, loss_ref.shape)
+
+
+def join(parts_ref, local_ref, sums_ref, grads_ref):
     group, qlen = grads_ref.shape[0], grads_ref.shape[1]
-    lane = iota((1, LANES), 1)
-    loss = jnp.zeros((1, 1), f32)
-    lses = []
-    for side in range(parts_ref.shape[0] // group):
-        parts = parts_ref[side * group : (side + 1) * group]
-        total, cross, kept = (pltpu.roll(parts, LANES - (k + 1) * group, 1) for k in range(3))
-        top = jnp.max(parts, axis=0, keepdims=True)
-        lse = top + jnp.log(jnp.sum(total * jnp.exp(parts - top), axis=0, keepdims=True))
-        agreed = jnp.sum(cross + kept * (parts - lse), axis=0, keepdims=True)
-        loss = loss - jnp.sum(jnp.where(lane < group, agreed, 0.0), axis=1, keepdims=True)
-        lses.append(lse)
-    loss_ref[...] = jnp.broadcast_to(loss, loss_ref.shape)
-    lse = lses[0]
-    for side in range(1, len(lses)):
-        lse = jnp.where(side_ref[0] == side, lses[side], lse)
-    factor = jnp.where(lane < group, jnp.exp(local_ref[0:1, :] - lse), 0.0)
+    shards = parts_ref.shape[0] // TOLD
+    own = lax.axis_index("query")
+    side = own // (lax.axis_size("query") // 2) * 2 + own % 2
+    lse = shared(parts_ref[pl.ds(pl.multiple_of(side * shards, 8), shards), :])[0]
+    factor = jnp.where(iota((1, LANES), 1) < group, jnp.exp(local_ref[0:1, :] - lse), 0.0)
     factors = jnp.transpose(jnp.broadcast_to(factor, (LANES, LANES)))
     for q in range(group):
         grads_ref[q] = sums_ref[q, :qlen] * factors[q : q + 1, :] - sums_ref[q, qlen:]
@@ -273,7 +281,7 @@
 
 def body(query_tokens, passage_tokens, passage_lengths, cand_shard, cand_local, teacher_scores):
     shards, groups = lax.axis_size("passage"), lax.axis_size("query")
-    me, own = lax.axis_index("passage"), lax.axis_index("query")
+    me = lax.axis_index("passage")
     group, cands = cand_local.shape
     qlen, dim = query_tokens.shape[1:]
     passages, plen, _ = passage_tokens.shape
@@ -290,15 +298,15 @@
             held((units, LANES), f32),
             held((1, LANES), f32),
         ),
-        [SMEM, VMEM, VMEM, VMEM, VMEM],
+        [VMEM, VMEM, VMEM, VMEM],
         int(2e9),
-    )(me.reshape(1), cand_shard.reshape(group, cands), cand_local, teacher_scores, lengths)
+    )(cand_shard.reshape(group, cands), cand_local, teacher_scores, lengths)
     weights, factors, local = call(
         score,
         (
             pltpu.HBM((units, SLOTS * qlen, plen), bf16),
             pltpu.HBM((units, LANES), f32),
-            held((PAIR * shards, LANES), f32),
+            held((TOLD * shards, LANES), f32),
         ),
         [SMEM, VMEM, VMEM, VMEM, VMEM, VMEM, VMEM, VMEM],
         int(4e9),
@@ -312,9 +320,10 @@
             pltpu.SemaphoreType.DMA((units // UNROLL + 1,)),
         ],
     )(table.reshape(-1), queries, passage_tokens, slot, count, mass, share, entropy)
-    pairs = [[g * shards + s for g in range(a, a + PAIR) for s in range(shards)] for a in range(0, groups, PAIR)]
+    told = [[a + c + h * groups // 2 for h in range(2) for c in range(2)] for a in range(0, groups // 2, 2)]
+    sets = [[g * shards + s for g in members for s in range(shards)] for members in told]
     parts = lax.all_to_all(
-        local.reshape(PAIR * shards, 1, LANES), ("query", "passage"), 0, 0, tiled=True, axis_index_groups=pairs
+        local.reshape(TOLD * shards, 1, LANES), ("query", "passage"), 0, 0, tiled=True, axis_index_groups=sets
     )
     (sums,) = call(
         terms_of,
@@ -329,15 +338,14 @@
             pltpu.SemaphoreType.DMA((units // UNROLL + 1,)),
         ],
     )(table.reshape(-1), in_hbm(weights), passage_tokens, in_hbm(factors))
-    grads, loss = call(
-        join,
-        (jax.ShapeDtypeStruct((group, qlen, dim), f32), jax.ShapeDtypeStruct((1, LANES), f32)),
-        [SMEM, VMEM, VMEM, VMEM],
-        int(1e9),
-    )((own % PAIR).reshape(1), parts.reshape(PAIR * shards, LANES), local, sums)
+    parts = parts.reshape(TOLD * shards, LANES)
+    (grads,) = call(
+        join, (jax.ShapeDtypeStruct((group, qlen, dim), f32),), [VMEM, VMEM, VMEM], int(1e9)
+    )(parts, local, sums)
+    (loss,) = call(losses, (jax.ShapeDtypeStruct((1, LANES), f32),), [VMEM], int(1e9))(parts)
     sent = lax.all_to_all(grads, "passage", 0, 0, tiled=True)
-    rings = [list(range(a, groups, PAIR)) for a in range(PAIR)]
-    loss = lax.psum(loss, "query", axis_index_groups=rings)
+    left = [list(members) for members in zip(*told)]
+    loss = lax.psum(loss, "query", axis_index_groups=left)
     query_grads = jnp.sum(sent, axis=0, keepdims=True)
     return (loss[0, 0] / (groups * group), query_grads)
 

time: 81.5 us -> 88.6 us (1.087)
  the two profiles are of different devices: /device:TPU:2 before, /device:TPU:1 now
where the time goes in v4:
time: 88.6 us; the launch traced here: 88 us
  starting transfers between devices  31.5 us (36%)
  waiting for transfers between devices  22.6 us (26%)
  Pallas kernels  17.6 us (20%)
  blocking collectives  9.92 us (11%)
  local copies, waits for them, and re-layouts  3.8 us (4%)
  between operations  1.87 us (2%)
    all_to_all x1, starting transfers between devices, body(): lax.all_to_all(local.reshape(TOLD * shards, 1, LANES), ('query', 'passage...  17.1 us
    all_to_all x1, starting transfers between devices, body(): lax.all_to_all(jnp.broadcast_to(query_tokens, (shards, qlen, dim)), 'pass...  10.5 us
    psum x1, blocking collectives, body(): loss = lax.psum(loss, 'query', axis_index_groups=left)  9.92 us
    all_to_all x1, waiting for transfers between devices, body(): lax.all_to_all(local.reshape(TOLD * shards, 1, LANES), ('query', 'passage...  8.78 us
    pallas_call x1, Pallas kernels, body(): call(score, (pltpu.HBM((units, SLOTS * qlen, plen), bf16), pltpu.HBM((uni...  8.21 us
    all_to_all x1, waiting for transfers between devices, body(): lax.all_to_all(jnp.broadcast_to(query_tokens, (shards, qlen, dim)), 'pass...  7.27 us
    all_to_all x1, waiting for transfers between devices, body(): sent = lax.all_to_all(grads, 'passage', 0, 0, tiled=True)  6.58 us
    pallas_call x1, Pallas kernels, body(): call(terms_of, (held((group + 1, 2 * qlen, dim), f32),), [SMEM, HBM, VMEM...  5.79 us
  transfers between devices with their start and end apart: 3, of which 3 were waited for; matrix products, arithmetic and copies ran while one was open for 1% of the time, Pallas kernels for 9%

profile of v4, /device:TPU:1, one launch (start us, length us, event | category | flops | bytes accessed | tf_op | source)
XLA Modules:
  0.0 88.0 jit_solution(15764026446785027770)
XLA Ops:
  0.6 0.0 copy-start
  0.6 1.4 %broadcast_in_dim.11 = bf16[32,32,128]{2,1,0:T(8,128)(2,1)} broadcast(bf16[32,128]{1,0:T(8,128)(2,1)} %bitcast.20), dimensions={1,2} | broadcast | bytes 270336 | tf_op jit(solution)/shard_map/broadcast_in_dim | solution.py:289
  2.1 10.5 %all-to-all-start = ((bf16[32,32,128]{2,1,0:T(8,128)(2,1)}), bf16[32,32,128]{2,1,0:T(8,128)(2,1)S(1)}, u32[]{:S(2)}, u32[]{:S(2)}) async-start(bf16[32,32,128]{2,1,0:T(8,128)(2,1)} %broadcast_in_dim.11), calls=%async_computation | async-start | bytes 524288 | tf_op jit(solution)/shard_map/all_to_all | solution.py:289
  12.6 0.8 copy.11
  13.4 0.0 copy-done
  13.4 0.1 dynamic-slice_bitcast_fusion.lengths_ref
  13.4 0.0 copy-start.2
  13.4 0.8 copy-done.2
  14.2 0.0 copy-start.3
  14.2 0.8 copy-done.3
  15.0 0.0 copy-start.1
  15.0 1.6 %shard_map.77 = (s32[16,128]{1,0:T(8,128)S(1)}, f32[176,128]{1,0:T(8,128)S(1)}, f32[176,128]{1,0:T(8,128)S(1)}, f32[176,128]{1,0:T(8,128)S(1)}, f32[176,128]{1,0:T(8,128)S(1)}, /*index=5*/f32[1,128]{1,0:T(1,128)S(1)}) custom-call(s32[32,256]{1,0:T(8,128)S(1)} %bitcast.16, s32[32,256]{1,0:T(8,128)S(1)} %copy-done.2, f32[32,256]{1,0:T(8,128)S(1)} %copy-done.3, ...), custom_call_target="tpu_custom_call" | custom-call | flops 2000000000 | bytes 20000000 | tf_op jit(solution)/shard_map/pallas_call | solution.py:291
  16.5 7.3 %all-to-all-done.query_ref = bf16[32,32,128]{2,1,0:T(8,128)(2,1)S(1)} async-done(((bf16[32,32,128]{2,1,0:T(8,128)(2,1)}), bf16[32,32,128]{2,1,0:T(8,128)(2,1)S(1)}, u32[]{:S(2)}, u32[]{:S(2)}) %all-to-all-start) | async-done | bytes 262176 | tf_op jit(solution)/shard_map/all_to_all | solution.py:289
  23.8 0.0 copy-done.1
  23.8 8.2 %shard_map.78 = (bf16[176,128,128]{2,1,0:T(8,128)(2,1)}, f32[176,128]{1,0:T(8,128)}, f32[128,128]{1,0:T(8,128)}) custom-call(s32[2048]{0:T(1024)S(1)} %bitcast.17, bf16[32,32,128]{2,1,0:T(8,128)(2,1)S(1)} %all-to-all-done.query_ref, bf16[64,128,128]{2,1,0:T(8,128)(2,1)S(1)} %copy-done.1, f32[176,128]{1,0:T(8,128)S(1)} %get-tuple-element.12.slot_ref, ...), custom_call_target="tpu_custom_call" | custom-call | flops 4000000000 | bytes 40000000 | tf_op jit(solution)/shard_map/pallas_call | solution.py:304
  32.0 17.1 %all-to-all-start.1 = ((f32[128,1,128]{2,1,0:T(1,128)}), f32[128,1,128]{2,1,0:T(1,128)S(1)}, u32[]{:S(2)}, u32[]{:S(2)}) async-start(f32[128,1,128]{2,1,0:T(1,128)} %bitcast.4), calls=%async_computation.1 | async-start | bytes 131072 | tf_op jit(solution)/shard_map/all_to_all | solution.py:325
  49.1 5.8 %shard_map.80.sums_ref = f32[33,64,128]{2,1,0:T(8,128)S(1)} custom-call(s32[2048]{0:T(1024)S(1)} %bitcast.18, bf16[176,128,128]{2,1,0:T(8,128)(2,1)} %get-tuple-element.18.weight_ref, bf16[64,128,128]{2,1,0:T(8,128)(2,1)S(1)} %copy-done.1, f32[176,128]{1,0:T(8,128)} %get-tuple-element.19.factor_ref), custom_call_target="tpu_custom_call" | custom-call | flops 4000000000 | bytes 40000000 | tf_op jit(solution)/shard_map/pallas_call | solution.py:328
  54.9 8.8 %all-to-all-done.1 = f32[128,1,128]{2,1,0:T(1,128)S(1)} async-done(((f32[128,1,128]{2,1,0:T(1,128)}), f32[128,1,128]{2,1,0:T(1,128)S(1)}, u32[]{:S(2)}, u32[]{:S(2)}) %all-to-all-start.1) | async-done | bytes 65568 | tf_op jit(solution)/shard_map/all_to_all | solution.py:325
  63.7 1.8 %shard_map.81 = f32[32,32,128]{2,1,0:T(8,128)} custom-call(f32[128,128]{1,0:T(8,128)S(1)} %bitcast.14, f32[128,128]{1,0:T(8,128)} %get-tuple-element.17.local_ref, f32[33,64,128]{2,1,0:T(8,128)S(1)} %shard_map.80.sums_ref), custom_call_target="tpu_custom_call" | custom-call | flops 1000000000 | bytes 10000000 | tf_op jit(solution)/shard_map/pallas_call | solution.py:342
  65.5 3.9 %all-to-all-start.2 = ((f32[32,32,128]{2,1,0:T(8,128)}), f32[32,32,128]{2,1,0:T(8,128)S(1)}, u32[]{:S(2)}, u32[]{:S(2)}) async-start(f32[32,32,128]{2,1,0:T(8,128)} %shard_map.81), calls=%async_computation.2 | async-start | bytes 1048576 | tf_op jit(solution)/shard_map/all_to_all | solution.py:346
  69.4 0.2 shard_map.79
  69.6 9.9 %psum.7 = f32[1,128]{1,0:T(1,128)S(1)} all-reduce(f32[1,128]{1,0:T(1,128)S(1)} %shard_map.79), channel_id=1, replica_groups={{0,64,128,192},{32,96,160,224},{256,320,384,448},{288,352,416,480},{1,6..., use_global_device_ids=true, to_apply=%region_0.0 | all-reduce | flops 128 | bytes 1024 | tf_op jit(solution)/shard_map/psum | solution.py:348
  79.6 6.6 %all-to-all-done.2 = f32[32,32,128]{2,1,0:T(8,128)S(1)} async-done(((f32[32,32,128]{2,1,0:T(8,128)}), f32[32,32,128]{2,1,0:T(8,128)S(1)}, u32[]{:S(2)}, u32[]{:S(2)}) %all-to-all-start.2) | async-done | bytes 524320 | tf_op jit(solution)/shard_map/all_to_all | solution.py:346
  86.2 0.6 reduce_sum.9
Async XLA Ops:
  0.6 12.7 %copy-start = (s32[2048]{0:T(1024)S(1)}, s32[2048]{0:T(1024)}, u32[]{:S(2)}) copy-start(s32[2048]{0:T(1024)} %param.8) | copy-start | bytes 24580
  2.1 21.7 %all-to-all-start = ((bf16[32,32,128]{2,1,0:T(8,128)(2,1)}), bf16[32,32,128]{2,1,0:T(8,128)(2,1)S(1)}, u32[]{:S(2)}, u32[]{:S(2)}) async-start(bf16[32,32,128]{2,1,0:T(8,128)(2,1)} %broadcast_in_dim.11), calls=%async_computation | async-start | bytes 524288 | tf_op jit(solution)/shard_map/all_to_all | solution.py:289
  13.4 0.8 copy-start.2
  14.2 0.8 copy-start.3
  15.0 8.8 %copy-start.1 = (bf16[64,128,128]{2,1,0:T(8,128)(2,1)S(1)}, bf16[64,128,128]{2,1,0:T(8,128)(2,1)}, u32[]{:S(2)}) copy-start(bf16[64,128,128]{2,1,0:T(8,128)(2,1)} %passage_ref.3) | copy-start | bytes 6291460
  32.0 31.7 %all-to-all-start.1 = ((f32[128,1,128]{2,1,0:T(1,128)}), f32[128,1,128]{2,1,0:T(1,128)S(1)}, u32[]{:S(2)}, u32[]{:S(2)}) async-start(f32[128,1,128]{2,1,0:T(1,128)} %bitcast.4), calls=%async_computation.1 | async-start | bytes 131072 | tf_op jit(solution)/shard_map/all_to_all | solution.py:325
  65.5 20.6 %all-to-all-start.2 = ((f32[32,32,128]{2,1,0:T(8,128)}), f32[32,32,128]{2,1,0:T(8,128)S(1)}, u32[]{:S(2)}, u32[]{:S(2)}) async-start(f32[32,32,128]{2,1,0:T(8,128)} %shard_map.81), calls=%async_computation.2 | async-start | bytes 1048576 | tf_op jit(solution)/shard_map/all_to_all | solution.py:346

commit v5 on v4

--- a/solution.py
+++ b/solution.py
@@ -8,11 +8,12 @@
 
 LANES = 128
 SLOTS = 4
+AHEAD = 16
 UNROLL = 8
 UNITS = 176
 PLEN = 128
 PADDED = 256
-TOLD = 4
+TOLD = 2
 FLOOR = -1e30
 NT = (((1,), (1,)), ((), ()))
 VMEM = pl.BlockSpec(memory_space=pltpu.VMEM)
@@ -119,38 +120,45 @@
     return k * PADDED
 
 
-def trips(table_ref):
-    return (table_ref[field(SLOTS + 2)] + (UNROLL - 1)) // UNROLL
+def trips(table_ref, size):
+    return (table_ref[field(SLOTS + 2)] + (size - 1)) // size
 
 
 def score(
     table_ref, query_ref, passage_ref, slot_ref, count_ref, mass_ref, share_ref, entropy_ref,
-    weight_ref, factor_ref, local_ref,
-    double_ref, row_ref, logits_ref, buffer_ref, scale_ref, cap_ref, sems,
+    weight_ref, factor_ref, local_ref, own_ref,
+    double_ref, row_ref, logits_ref, buffer_ref, scale_ref, cap_ref, turned_ref, sems,
 ):
     group, qlen = query_ref.shape[0], query_ref.shape[1]
     units, columns, plen = weight_ref.shape
     double_ref[:group] = query_ref[...] * 2
     double_ref[group] = jnp.zeros(double_ref.shape[1:], bf16)
     row_ref[...] = jnp.zeros(row_ref.shape, f32)
-    logits_ref[...] = jnp.zeros(logits_ref.shape, f32)
     for part in range(8):
         cap_ref[part] = jnp.where(iota((2 * plen, columns), 0) < plen + part, -FLOOR, FLOOR)
-    rounds = trips(table_ref)
+    rounds = trips(table_ref, AHEAD)
 
     def out(t):
-        first = pl.multiple_of(t * UNROLL, UNROLL)
+        first = pl.multiple_of(t * AHEAD, AHEAD)
         return pltpu.make_async_copy(
-            buffer_ref.at[pl.ds(first + UNROLL, UNROLL)], weight_ref.at[pl.ds(first, UNROLL)], sems.at[t]
+            buffer_ref.at[pl.ds(first + AHEAD, AHEAD)], weight_ref.at[pl.ds(first, AHEAD)], sems.at[t]
         )
 
+    def turn(u):
+        tokens = [double_ref[table_ref[field(k) + u]] for k in range(SLOTS)]
+        return jnp.transpose(jnp.concatenate(tokens, axis=0))
+
+    for j in range(AHEAD):
+        turned_ref[j] = turn(j)
+
     def some(t, carry):
-        for j in range(UNROLL):
-            u = t * UNROLL + j
+        for j in range(AHEAD):
+            u = t * AHEAD + j
             old = logits_ref[j]
             p = table_ref[field(SLOTS) + u]
-            tokens = jnp.concatenate([double_ref[table_ref[field(k) + u]] for k in range(SLOTS)], axis=0)
-            logits = lax.dot_general(passage_ref[p], tokens, NT, preferred_element_type=f32)
+            tokens = turned_ref[j]
+            turned_ref[j] = turn(u + AHEAD)
+            logits = jnp.dot(passage_ref[p], tokens, preferred_element_type=f32)
             start = pl.multiple_of(table_ref[field(SLOTS + 1) + u], 8)
             logits_ref[j] = jnp.minimum(logits, cap_ref[table_ref[field(SLOTS + 3) + u], pl.ds(start, plen), :])
             top = jnp.max(old, axis=0, keepdims=True)
@@ -167,7 +175,7 @@
 
     lax.fori_loop(0, rounds + 1, some, 0)
     same = iota((columns, LANES), 0) // qlen == iota((columns, LANES), 1)
-    rows = row_ref[pl.ds(UNROLL, units), :]
+    rows = row_ref[pl.ds(AHEAD, units), :]
     summed = jnp.dot(rows, jnp.where(same, 0.5, 0.0), preferred_element_type=f32, precision=lax.Precision.HIGHEST)
     slot, count, mass = slot_ref[...], count_ref[...], mass_ref[...]
     scores = jnp.zeros((units, LANES), f32)
@@ -182,7 +190,7 @@
     for k in range(SLOTS):
         scale = jnp.where(wide == k, jnp.sum(jnp.where(slot == float(k), student, 0.0), axis=1, keepdims=True), scale)
     scale_ref[...] = scale
-    factors = pltpu.make_async_copy(scale_ref, factor_ref, sems.at[units // UNROLL])
+    factors = pltpu.make_async_copy(scale_ref, factor_ref, sems.at[units // AHEAD])
     factors.start()
     total = jnp.sum(student, axis=0, keepdims=True)
     lane = iota((1, LANES), 1)
@@ -193,6 +201,7 @@
         moved = pltpu.roll(jnp.broadcast_to(part, (8, LANES)), (k + 1) * group, 1)[0:1]
         packed = jnp.where(lane // group == k + 1, moved, packed)
     local_ref[...] = jnp.broadcast_to(packed, local_ref.shape)
+    own_ref[...] = jnp.broadcast_to(packed, own_ref.shape)
 
     def finish(t, carry):
         out(t).wait()
@@ -205,7 +214,7 @@
 def terms_of(table_ref, weight_ref, passage_ref, factor_ref, sums_ref, scale_ref, spread_ref, grads_ref, buffer_ref, sems):
     qlen = sums_ref.shape[1] // 2
     units = weight_ref.shape[0]
-    rounds = trips(table_ref)
+    rounds = trips(table_ref, UNROLL)
     factors = pltpu.make_async_copy(factor_ref, scale_ref, sems.at[units // UNROLL])
     factors.start()
 
@@ -267,13 +276,12 @@
     loss_ref[...] = jnp.broadcast_to(loss, loss_ref.shape)
 
 
-def join(parts_ref, local_ref, sums_ref, grads_ref):
+def join(parts_ref, own_ref, sums_ref, grads_ref):
     group, qlen = grads_ref.shape[0], grads_ref.shape[1]
     shards = parts_ref.shape[0] // TOLD
-    own = lax.axis_index("query")
-    side = own // (lax.axis_size("query") // 2) * 2 + own % 2
+    side = lax.axis_index("query") % TOLD
     lse = shared(parts_ref[pl.ds(pl.multiple_of(side * shards, 8), shards), :])[0]
-    factor = jnp.where(iota((1, LANES), 1) < group, jnp.exp(local_ref[0:1, :] - lse), 0.0)
+    factor = jnp.where(iota((1, LANES), 1) < group, jnp.exp(own_ref[0:1, :] - lse), 0.0)
     factors = jnp.transpose(jnp.broadcast_to(factor, (LANES, LANES)))
     for q in range(group):
         grads_ref[q] = sums_ref[q, :qlen] * factors[q : q + 1, :] - sums_ref[q, qlen:]
@@ -301,26 +309,28 @@
         [VMEM, VMEM, VMEM, VMEM],
         int(2e9),
     )(cand_shard.reshape(group, cands), cand_local, teacher_scores, lengths)
-    weights, factors, local = call(
+    weights, factors, local, own = call(
         score,
         (
             pltpu.HBM((units, SLOTS * qlen, plen), bf16),
             pltpu.HBM((units, LANES), f32),
             held((TOLD * shards, LANES), f32),
+            held((8, LANES), f32),
         ),
         [SMEM, VMEM, VMEM, VMEM, VMEM, VMEM, VMEM, VMEM],
         int(4e9),
         [
             pltpu.VMEM((group + 1, qlen, dim), bf16),
-            pltpu.VMEM((UNROLL + units, LANES), f32),
-            pltpu.VMEM((UNROLL, plen, SLOTS * qlen), f32),
-            pltpu.VMEM((UNROLL + units, SLOTS * qlen, plen), bf16),
+            pltpu.VMEM((AHEAD + units, LANES), f32),
+            pltpu.VMEM((AHEAD, plen, SLOTS * qlen), f32),
+            pltpu.VMEM((AHEAD + units, SLOTS * qlen, plen), bf16),
             pltpu.VMEM((units, LANES), f32),
             pltpu.VMEM((8, 2 * plen, SLOTS * qlen), f32),
-            pltpu.SemaphoreType.DMA((units // UNROLL + 1,)),
+            pltpu.VMEM((AHEAD, dim, SLOTS * qlen), bf16),
+            pltpu.SemaphoreType.DMA((units // AHEAD + 1,)),
         ],
     )(table.reshape(-1), queries, passage_tokens, slot, count, mass, share, entropy)
-    told = [[a + c + h * groups // 2 for h in range(2) for c in range(2)] for a in range(0, groups // 2, 2)]
+    told = [list(range(a, a + TOLD)) for a in range(0, groups, TOLD)]
     sets = [[g * shards + s for g in members for s in range(shards)] for members in told]
     parts = lax.all_to_all(
         local.reshape(TOLD * shards, 1, LANES), ("query", "passage"), 0, 0, tiled=True, axis_index_groups=sets
@@ -341,7 +351,7 @@
     parts = parts.reshape(TOLD * shards, LANES)
     (grads,) = call(
         join, (jax.ShapeDtypeStruct((group, qlen, dim), f32),), [VMEM, VMEM, VMEM], int(1e9)
-    )(parts, local, sums)
+    )(parts, own, sums)
     (loss,) = call(losses, (jax.ShapeDtypeStruct((1, LANES), f32),), [VMEM], int(1e9))(parts)
     sent = lax.all_to_all(grads, "passage", 0, 0, tiled=True)
     left = [list(members) for members in zip(*told)]

time: 88.6 us -> 80.7 us (0.911)
  the two profiles are of different devices: /device:TPU:1 before, /device:TPU:2 now
where the time goes in v5:
time: 80.7 us; the launch traced here: 80.1 us
  starting transfers between devices  26.5 us (33%)
  blocking collectives  23.5 us (29%)
  Pallas kernels  12.4 us (15%)
  waiting for transfers between devices  11.5 us (14%)
  local copies, waits for them, and re-layouts  3.8 us (5%)
  between operations  1.87 us (2%)
    psum x1, blocking collectives, body(): loss = lax.psum(loss, 'query', axis_index_groups=left)  23.5 us
    all_to_all x1, starting transfers between devices, body(): lax.all_to_all(jnp.broadcast_to(query_tokens, (shards, qlen, dim)), 'pass...  10.2 us
    all_to_all x1, starting transfers between devices, body(): lax.all_to_all(local.reshape(TOLD * shards, 1, LANES), ('query', 'passage...  8.44 us
    all_to_all x1, starting transfers between devices, body(): sent = lax.all_to_all(grads, 'passage', 0, 0, tiled=True)  7.79 us
    all_to_all x1, waiting for transfers between devices, body(): lax.all_to_all(jnp.broadcast_to(query_tokens, (shards, qlen, dim)), 'pass...  7.29 us
    pallas_call x1, Pallas kernels, body(): call(score, (pltpu.HBM((units, SLOTS * qlen, plen), bf16), pltpu.HBM((uni...  5.55 us
    all_to_all x1, waiting for transfers between devices, body(): lax.all_to_all(local.reshape(TOLD * shards, 1, LANES), ('query', 'passage...  4.18 us
    pallas_call x1, Pallas kernels, body(): call(terms_of, (held((group + 1, 2 * qlen, dim), f32),), [SMEM, HBM, VMEM...  4.08 us
  transfers between devices with their start and end apart: 3, of which 2 were waited for; matrix products, arithmetic and copies ran while one was open for 1% of the time, Pallas kernels for 7%

profile of v5, /device:TPU:2, one launch (start us, length us, event | category | flops | bytes accessed | tf_op | source)
XLA Modules:
  0.0 80.1 jit_solution(9921444254326717289)
XLA Ops:
  0.6 0.0 copy-start
  0.6 1.4 %broadcast_in_dim.11 = bf16[32,32,128]{2,1,0:T(8,128)(2,1)} broadcast(bf16[32,128]{1,0:T(8,128)(2,1)} %bitcast.20), dimensions={1,2} | broadcast | bytes 270336 | tf_op jit(solution)/shard_map/broadcast_in_dim | solution.py:297
  2.1 10.2 %all-to-all-start = ((bf16[32,32,128]{2,1,0:T(8,128)(2,1)}), bf16[32,32,128]{2,1,0:T(8,128)(2,1)S(1)}, u32[]{:S(2)}, u32[]{:S(2)}) async-start(bf16[32,32,128]{2,1,0:T(8,128)(2,1)} %broadcast_in_dim.11), calls=%async_computation | async-start | bytes 524288 | tf_op jit(solution)/shard_map/all_to_all | solution.py:297
  12.3 0.8 copy.11
  13.1 0.0 copy-done
  13.1 0.1 dynamic-slice_bitcast_fusion.lengths_ref
  13.2 0.0 copy-start.2
  13.2 0.8 copy-done.2
  13.9 0.0 copy-start.3
  13.9 0.8 copy-done.3
  14.7 0.0 copy-start.1
  14.7 1.6 %shard_map.77 = (s32[16,128]{1,0:T(8,128)S(1)}, f32[176,128]{1,0:T(8,128)S(1)}, f32[176,128]{1,0:T(8,128)S(1)}, f32[176,128]{1,0:T(8,128)S(1)}, f32[176,128]{1,0:T(8,128)S(1)}, /*index=5*/f32[1,128]{1,0:T(1,128)S(1)}) custom-call(s32[32,256]{1,0:T(8,128)S(1)} %bitcast.16, s32[32,256]{1,0:T(8,128)S(1)} %copy-done.2, f32[32,256]{1,0:T(8,128)S(1)} %copy-done.3, ...), custom_call_target="tpu_custom_call" | custom-call | flops 2000000000 | bytes 20000000 | tf_op jit(solution)/shard_map/pallas_call | solution.py:299
  16.3 7.3 %all-to-all-done.query_ref = bf16[32,32,128]{2,1,0:T(8,128)(2,1)S(1)} async-done(((bf16[32,32,128]{2,1,0:T(8,128)(2,1)}), bf16[32,32,128]{2,1,0:T(8,128)(2,1)S(1)}, u32[]{:S(2)}, u32[]{:S(2)}) %all-to-all-start) | async-done | bytes 262176 | tf_op jit(solution)/shard_map/all_to_all | solution.py:297
  23.6 0.0 copy-done.1
  23.6 5.5 %shard_map.78 = (bf16[176,128,128]{2,1,0:T(8,128)(2,1)}, f32[176,128]{1,0:T(8,128)}, f32[64,128]{1,0:T(8,128)}, f32[8,128]{1,0:T(8,128)S(1)}) custom-call(s32[2048]{0:T(1024)S(1)} %bitcast.17, bf16[32,32,128]{2,1,0:T(8,128)(2,1)S(1)} %all-to-all-done.query_ref, bf16[64,128,128]{2,1,0:T(8,128)(2,1)S(1)} %copy-done.1, ...), custom_call_target="tpu_custom_call" | custom-call | flops 4000000000 | bytes 40000000 | tf_op jit(solution)/shard_map/pallas_call | solution.py:312
  29.1 8.4 %all-to-all-start.1 = ((f32[64,1,128]{2,1,0:T(1,128)}), f32[64,1,128]{2,1,0:T(1,128)S(1)}, u32[]{:S(2)}, u32[]{:S(2)}) async-start(f32[64,1,128]{2,1,0:T(1,128)} %bitcast.4), calls=%async_computation.1 | async-start | bytes 65536 | tf_op jit(solution)/shard_map/all_to_all | solution.py:335
  37.6 4.1 %shard_map.80.sums_ref = f32[33,64,128]{2,1,0:T(8,128)S(1)} custom-call(s32[2048]{0:T(1024)S(1)} %bitcast.18, bf16[176,128,128]{2,1,0:T(8,128)(2,1)} %get-tuple-element.20.weight_ref, bf16[64,128,128]{2,1,0:T(8,128)(2,1)S(1)} %copy-done.1, f32[176,128]{1,0:T(8,128)} %get-tuple-element.21.factor_ref), custom_call_target="tpu_custom_call" | custom-call | flops 4000000000 | bytes 40000000 | tf_op jit(solution)/shard_map/pallas_call | solution.py:338
  41.6 4.2 %all-to-all-done.1 = f32[64,1,128]{2,1,0:T(1,128)S(1)} async-done(((f32[64,1,128]{2,1,0:T(1,128)}), f32[64,1,128]{2,1,0:T(1,128)S(1)}, u32[]{:S(2)}, u32[]{:S(2)}) %all-to-all-start.1) | async-done | bytes 32800 | tf_op jit(solution)/shard_map/all_to_all | solution.py:335
  45.8 1.0 %shard_map.81 = f32[32,32,128]{2,1,0:T(8,128)} custom-call(f32[64,128]{1,0:T(8,128)S(1)} %bitcast.14, f32[8,128]{1,0:T(8,128)S(1)} %get-tuple-element.19.own_ref, f32[33,64,128]{2,1,0:T(8,128)S(1)} %shard_map.80.sums_ref), custom_call_target="tpu_custom_call" | custom-call | flops 1000000000 | bytes 10000000 | tf_op jit(solution)/shard_map/pallas_call | solution.py:352
  46.8 7.8 %all-to-all-start.2 = ((f32[32,32,128]{2,1,0:T(8,128)}), f32[32,32,128]{2,1,0:T(8,128)S(1)}, u32[]{:S(2)}, u32[]{:S(2)}) async-start(f32[32,32,128]{2,1,0:T(8,128)} %shard_map.81), calls=%async_computation.2 | async-start | bytes 1048576 | tf_op jit(solution)/shard_map/all_to_all | solution.py:356
  54.6 0.2 shard_map.79
  54.8 23.5 %psum.7 = f32[1,128]{1,0:T(1,128)S(1)} all-reduce(f32[1,128]{1,0:T(1,128)S(1)} %shard_map.79), channel_id=1, replica_groups={{0,64,128,192,256,320,384,448},{32,96,160,224,288,352,416,480},{1,65,12..., use_global_device_ids=true, to_apply=%region_0.0 | all-reduce | flops 128 | bytes 1024 | tf_op jit(solution)/shard_map/psum | solution.py:358
  78.3 0.0 all-to-all-done.2
  78.3 0.7 reduce_sum.9
Async XLA Ops:
  0.6 12.5 %copy-start = (s32[2048]{0:T(1024)S(1)}, s32[2048]{0:T(1024)}, u32[]{:S(2)}) copy-start(s32[2048]{0:T(1024)} %param.8) | copy-start | bytes 24580
  2.1 21.5 %all-to-all-start = ((bf16[32,32,128]{2,1,0:T(8,128)(2,1)}), bf16[32,32,128]{2,1,0:T(8,128)(2,1)S(1)}, u32[]{:S(2)}, u32[]{:S(2)}) async-start(bf16[32,32,128]{2,1,0:T(8,128)(2,1)} %broadcast_in_dim.11), calls=%async_computation | async-start | bytes 524288 | tf_op jit(solution)/shard_map/all_to_all | solution.py:297
  13.2 0.8 copy-start.2
  13.9 0.8 copy-start.3
  14.7 8.9 %copy-start.1 = (bf16[64,128,128]{2,1,0:T(8,128)(2,1)S(1)}, bf16[64,128,128]{2,1,0:T(8,128)(2,1)}, u32[]{:S(2)}) copy-start(bf16[64,128,128]{2,1,0:T(8,128)(2,1)} %passage_ref.3) | copy-start | bytes 6291460
  29.1 16.7 %all-to-all-start.1 = ((f32[64,1,128]{2,1,0:T(1,128)}), f32[64,1,128]{2,1,0:T(1,128)S(1)}, u32[]{:S(2)}, u32[]{:S(2)}) async-start(f32[64,1,128]{2,1,0:T(1,128)} %bitcast.4), calls=%async_computation.1 | async-start | bytes 65536 | tf_op jit(solution)/shard_map/all_to_all | solution.py:335
  46.8 31.5 %all-to-all-start.2 = ((f32[32,32,128]{2,1,0:T(8,128)}), f32[32,32,128]{2,1,0:T(8,128)S(1)}, u32[]{:S(2)}, u32[]{:S(2)}) async-start(f32[32,32,128]{2,1,0:T(8,128)} %shard_map.81), calls=%async_computation.2 | async-start | bytes 1048576 | tf_op jit(solution)/shard_map/all_to_all | solution.py:356

commit v6 on v5

--- a/solution.py
+++ b/solution.py
@@ -13,7 +13,7 @@
 UNITS = 176
 PLEN = 128
 PADDED = 256
-TOLD = 2
+TOLD = 4
 FLOOR = -1e30
 NT = (((1,), (1,)), ((), ()))
 VMEM = pl.BlockSpec(memory_space=pltpu.VMEM)
@@ -265,23 +265,21 @@
     return lse, cross, kept
 
 
-def losses(parts_ref, loss_ref):
+def join(parts_ref, own_ref, sums_ref, grads_ref, loss_ref):
+    group, qlen = grads_ref.shape[0], grads_ref.shape[1]
     shards = parts_ref.shape[0] // TOLD
+    mine = lax.axis_index("query") % TOLD
+    lane = iota((1, LANES), 1)
     loss = jnp.zeros((1, 1), f32)
+    lse = jnp.zeros((1, LANES), f32)
     for side in range(TOLD):
         parts = parts_ref[side * shards : (side + 1) * shards]
-        lse, cross, kept = shared(parts)
-        agreed = jnp.sum(cross + kept * (parts - lse), axis=0, keepdims=True)
-        loss = loss - jnp.sum(jnp.where(iota((1, LANES), 1) < LANES // 4, agreed, 0.0), axis=1, keepdims=True)
+        found, cross, kept = shared(parts)
+        agreed = jnp.sum(cross + kept * (parts - found), axis=0, keepdims=True)
+        loss = loss - jnp.sum(jnp.where(lane < group, agreed, 0.0), axis=1, keepdims=True)
+        lse = jnp.where(mine == side, found, lse)
     loss_ref[...] = jnp.broadcast_to(loss, loss_ref.shape)
-
-
-def join(parts_ref, own_ref, sums_ref, grads_ref):
-    group, qlen = grads_ref.shape[0], grads_ref.shape[1]
-    shards = parts_ref.shape[0] // TOLD
-    side = lax.axis_index("query") % TOLD
-    lse = shared(parts_ref[pl.ds(pl.multiple_of(side * shards, 8), shards), :])[0]
-    factor = jnp.where(iota((1, LANES), 1) < group, jnp.exp(own_ref[0:1, :] - lse), 0.0)
+    factor = jnp.where(lane < group, jnp.exp(own_ref[0:1, :] - lse), 0.0)
     factors = jnp.transpose(jnp.broadcast_to(factor, (LANES, LANES)))
     for q in range(group):
         grads_ref[q] = sums_ref[q, :qlen] * factors[q : q + 1, :] - sums_ref[q, qlen:]
@@ -349,13 +347,15 @@
         ],
     )(table.reshape(-1), in_hbm(weights), passage_tokens, in_hbm(factors))
     parts = parts.reshape(TOLD * shards, LANES)
-    (grads,) = call(
-        join, (jax.ShapeDtypeStruct((group, qlen, dim), f32),), [VMEM, VMEM, VMEM], int(1e9)
+    grads, loss = call(
+        join,
+        (jax.ShapeDtypeStruct((group, qlen, dim), f32), jax.ShapeDtypeStruct((1, LANES), f32)),
+        [VMEM, VMEM, VMEM],
+        int(1e9),
     )(parts, own, sums)
-    (loss,) = call(losses, (jax.ShapeDtypeStruct((1, LANES), f32),), [VMEM], int(1e9))(parts)
     sent = lax.all_to_all(grads, "passage", 0, 0, tiled=True)
     left = [list(members) for members in zip(*told)]
-    loss = lax.psum(loss, "query", axis_index_groups=left)
+    loss = jnp.sum(lax.all_gather(loss, "query", axis=0, tiled=True, axis_index_groups=left), axis=0, keepdims=True)
     query_grads = jnp.sum(sent, axis=0, keepdims=True)
     return (loss[0, 0] / (groups * group), query_grads)
 

time: 80.7 us -> 77.2 us (0.957)
  the two profiles are of different devices: /device:TPU:2 before, /device:TPU:1 now
where the time goes in v6:
time: 77.2 us; the launch traced here: 76.4 us
  starting transfers between devices  24.7 us (32%)
  Pallas kernels  17.6 us (23%)
  waiting for transfers between devices  13.9 us (18%)
  blocking collectives  13.9 us (18%)
  local copies, waits for them, and re-layouts  3.8 us (5%)
  between operations  1.87 us (2%)
    all_gather x1, blocking collectives, body(): lax.all_gather(loss, 'query', axis=0, tiled=True, axis_index_groups=left)  13.9 us
    all_to_all x1, starting transfers between devices, body(): lax.all_to_all(jnp.broadcast_to(query_tokens, (shards, qlen, dim)), 'pass...  10.5 us
    all_to_all x1, starting transfers between devices, body(): lax.all_to_all(local.reshape(TOLD * shards, 1, LANES), ('query', 'passage...  9.1 us
    pallas_call x1, Pallas kernels, body(): call(score, (pltpu.HBM((units, SLOTS * qlen, plen), bf16), pltpu.HBM((uni...  8.19 us
    all_to_all x1, waiting for transfers between devices, body(): lax.all_to_all(jnp.broadcast_to(query_tokens, (shards, qlen, dim)), 'pass...  7.27 us
    pallas_call x1, Pallas kernels, body(): call(terms_of, (held((group + 1, 2 * qlen, dim), f32),), [SMEM, HBM, VMEM...  6.8 us
    all_to_all x1, starting transfers between devices, body(): sent = lax.all_to_all(grads, 'passage', 0, 0, tiled=True)  5.08 us
    all_to_all x1, waiting for transfers between devices, body(): lax.all_to_all(local.reshape(TOLD * shards, 1, LANES), ('query', 'passage...  3.84 us
  transfers between devices with their start and end apart: 3, of which 3 were waited for; matrix products, arithmetic and copies ran while one was open for 1% of the time, Pallas kernels for 11%

profile of v6, /device:TPU:1, one launch (start us, length us, event | category | flops | bytes accessed | tf_op | source)
XLA Modules:
  0.0 76.4 jit_solution(13774980925868060618)
XLA Ops:
  0.6 0.0 copy-start
  0.6 1.4 %broadcast_in_dim.14 = bf16[32,32,128]{2,1,0:T(8,128)(2,1)} broadcast(bf16[32,128]{1,0:T(8,128)(2,1)} %bitcast.22), dimensions={1,2} | broadcast | bytes 270336 | tf_op jit(solution)/shard_map/broadcast_in_dim | solution.py:295
  2.1 10.5 %all-to-all-start = ((bf16[32,32,128]{2,1,0:T(8,128)(2,1)}), bf16[32,32,128]{2,1,0:T(8,128)(2,1)S(1)}, u32[]{:S(2)}, u32[]{:S(2)}) async-start(bf16[32,32,128]{2,1,0:T(8,128)(2,1)} %broadcast_in_dim.14), calls=%async_computation | async-start | bytes 524288 | tf_op jit(solution)/shard_map/all_to_all | solution.py:295
  12.6 0.8 copy.11
  13.4 0.0 copy-done
  13.4 0.1 dynamic-slice_bitcast_fusion.lengths_ref
  13.4 0.0 copy-start.2
  13.4 0.8 copy-done.2
  14.2 0.0 copy-start.3
  14.2 0.8 copy-done.3
  15.0 0.0 copy-start.1
  15.0 1.6 %shard_map.77 = (s32[16,128]{1,0:T(8,128)S(1)}, f32[176,128]{1,0:T(8,128)S(1)}, f32[176,128]{1,0:T(8,128)S(1)}, f32[176,128]{1,0:T(8,128)S(1)}, f32[176,128]{1,0:T(8,128)S(1)}, /*index=5*/f32[1,128]{1,0:T(1,128)S(1)}) custom-call(s32[32,256]{1,0:T(8,128)S(1)} %bitcast.17, s32[32,256]{1,0:T(8,128)S(1)} %copy-done.2, f32[32,256]{1,0:T(8,128)S(1)} %copy-done.3, ...), custom_call_target="tpu_custom_call" | custom-call | flops 2000000000 | bytes 20000000 | tf_op jit(solution)/shard_map/pallas_call | solution.py:297
  16.5 7.3 %all-to-all-done.query_ref = bf16[32,32,128]{2,1,0:T(8,128)(2,1)S(1)} async-done(((bf16[32,32,128]{2,1,0:T(8,128)(2,1)}), bf16[32,32,128]{2,1,0:T(8,128)(2,1)S(1)}, u32[]{:S(2)}, u32[]{:S(2)}) %all-to-all-start) | async-done | bytes 262176 | tf_op jit(solution)/shard_map/all_to_all | solution.py:295
  23.8 0.0 copy-done.1
  23.8 8.2 %shard_map.78 = (bf16[176,128,128]{2,1,0:T(8,128)(2,1)}, f32[176,128]{1,0:T(8,128)}, f32[128,128]{1,0:T(8,128)}, f32[8,128]{1,0:T(8,128)S(1)}) custom-call(s32[2048]{0:T(1024)S(1)} %bitcast.19, bf16[32,32,128]{2,1,0:T(8,128)(2,1)S(1)} %all-to-all-done.query_ref, bf16[64,128,128]{2,1,0:T(8,128)(2,1)S(1)} %copy-done.1, ...), custom_call_target="tpu_custom_call" | custom-call | flops 4000000000 | bytes 40000000 | tf_op jit(solution)/shard_map/pallas_call | solution.py:310
  32.0 9.1 %all-to-all-start.1 = ((f32[128,1,128]{2,1,0:T(1,128)}), f32[128,1,128]{2,1,0:T(1,128)S(1)}, u32[]{:S(2)}, u32[]{:S(2)}) async-start(f32[128,1,128]{2,1,0:T(1,128)} %bitcast.4), calls=%async_computation.1 | async-start | bytes 131072 | tf_op jit(solution)/shard_map/all_to_all | solution.py:333
  41.1 6.8 %shard_map.79.sums_ref = f32[33,64,128]{2,1,0:T(8,128)S(1)} custom-call(s32[2048]{0:T(1024)S(1)} %bitcast.20, bf16[176,128,128]{2,1,0:T(8,128)(2,1)} %get-tuple-element.22.weight_ref, bf16[64,128,128]{2,1,0:T(8,128)(2,1)S(1)} %copy-done.1, f32[176,128]{1,0:T(8,128)} %get-tuple-element.23.factor_ref), custom_call_target="tpu_custom_call" | custom-call | flops 4000000000 | bytes 40000000 | tf_op jit(solution)/shard_map/pallas_call | solution.py:336
  47.9 3.8 %all-to-all-done.1 = f32[128,1,128]{2,1,0:T(1,128)S(1)} async-done(((f32[128,1,128]{2,1,0:T(1,128)}), f32[128,1,128]{2,1,0:T(1,128)S(1)}, u32[]{:S(2)}, u32[]{:S(2)}) %all-to-all-start.1) | async-done | bytes 65568 | tf_op jit(solution)/shard_map/all_to_all | solution.py:333
  51.7 1.1 %shard_map.80 = (f32[32,32,128]{2,1,0:T(8,128)}, f32[1,128]{1,0:T(1,128)S(1)}) custom-call(f32[128,128]{1,0:T(8,128)S(1)} %bitcast.16, f32[8,128]{1,0:T(8,128)S(1)} %get-tuple-element.21.own_ref, f32[33,64,128]{2,1,0:T(8,128)S(1)} %shard_map.79.sums_ref), custom_call_target="tpu_custom_call" | custom-call | flops 1000000000 | bytes 10000000 | tf_op jit(solution)/shard_map/pallas_call | solution.py:350
  52.8 5.1 %all-to-all-start.2 = ((f32[32,32,128]{2,1,0:T(8,128)}), f32[32,32,128]{2,1,0:T(8,128)S(1)}, u32[]{:S(2)}, u32[]{:S(2)}) async-start(f32[32,32,128]{2,1,0:T(8,128)} %get-tuple-element.25), calls=%async_computation.2 | async-start | bytes 1048576 | tf_op jit(solution)/shard_map/all_to_all | solution.py:356
  57.9 13.9 %all-gather = f32[4,1,128]{2,1,0:T(1,128)S(1)} all-gather(f32[1,1,128]{2,1,0:T(1,128)S(1)} %bitcast.18), channel_id=1, replica_groups={{0,128,256,384},{32,160,288,416},{64,192,320,448},{96,224,352,480},{1,1..., dimensions={0}, use_global_device_ids=true | all-gather | bytes 2560 | tf_op jit(solution)/shard_map/all_gather | solution.py:358
  71.9 2.8 %all-to-all-done.2 = f32[32,32,128]{2,1,0:T(8,128)S(1)} async-done(((f32[32,32,128]{2,1,0:T(8,128)}), f32[32,32,128]{2,1,0:T(8,128)S(1)}, u32[]{:S(2)}, u32[]{:S(2)}) %all-to-all-start.2) | async-done | bytes 524320 | tf_op jit(solution)/shard_map/all_to_all | solution.py:356
  74.6 0.6 reduce_sum.19
  (1 shorter events, 0.0 us)
Async XLA Ops:
  0.6 12.7 %copy-start = (s32[2048]{0:T(1024)S(1)}, s32[2048]{0:T(1024)}, u32[]{:S(2)}) copy-start(s32[2048]{0:T(1024)} %param.8) | copy-start | bytes 24580
  2.1 21.7 %all-to-all-start = ((bf16[32,32,128]{2,1,0:T(8,128)(2,1)}), bf16[32,32,128]{2,1,0:T(8,128)(2,1)S(1)}, u32[]{:S(2)}, u32[]{:S(2)}) async-start(bf16[32,32,128]{2,1,0:T(8,128)(2,1)} %broadcast_in_dim.14), calls=%async_computation | async-start | bytes 524288 | tf_op jit(solution)/shard_map/all_to_all | solution.py:295
  13.4 0.8 copy-start.2
  14.2 0.8 copy-start.3
  15.0 8.8 %copy-start.1 = (bf16[64,128,128]{2,1,0:T(8,128)(2,1)S(1)}, bf16[64,128,128]{2,1,0:T(8,128)(2,1)}, u32[]{:S(2)}) copy-start(bf16[64,128,128]{2,1,0:T(8,128)(2,1)} %passage_ref.3) | copy-start | bytes 6291460
  32.0 19.8 %all-to-all-start.1 = ((f32[128,1,128]{2,1,0:T(1,128)}), f32[128,1,128]{2,1,0:T(1,128)S(1)}, u32[]{:S(2)}, u32[]{:S(2)}) async-start(f32[128,1,128]{2,1,0:T(1,128)} %bitcast.4), calls=%async_computation.1 | async-start | bytes 131072 | tf_op jit(solution)/shard_map/all_to_all | solution.py:333
  52.8 21.8 %all-to-all-start.2 = ((f32[32,32,128]{2,1,0:T(8,128)}), f32[32,32,128]{2,1,0:T(8,128)S(1)}, u32[]{:S(2)}, u32[]{:S(2)}) async-start(f32[32,32,128]{2,1,0:T(8,128)} %get-tuple-element.25), calls=%async_computation.2 | async-start | bytes 1048576 | tf_op jit(solution)/shard_map/all_to_all | solution.py:356

commit v7 on v6

--- a/solution.py
+++ b/solution.py
@@ -42,6 +42,11 @@
         compiler_params=pltpu.CompilerParams(vmem_limit_bytes=24 * 1024 * 1024),
         cost_estimate=pl.CostEstimate(flops=cost, bytes_accessed=cost // 100, transcendentals=0),
     )
+
+
+def turns(shards):
+    rows = shards // 4
+    return [4 * (3 * row % rows) + column for column in range(4) for row in range(rows)]
 
 
 def iota(shape, axis):
@@ -281,8 +286,8 @@
     loss_ref[...] = jnp.broadcast_to(loss, loss_ref.shape)
     factor = jnp.where(lane < group, jnp.exp(own_ref[0:1, :] - lse), 0.0)
     factors = jnp.transpose(jnp.broadcast_to(factor, (LANES, LANES)))
-    for q in range(group):
-        grads_ref[q] = sums_ref[q, :qlen] * factors[q : q + 1, :] - sums_ref[q, qlen:]
+    for place, q in enumerate(turns(group)):
+        grads_ref[place] = sums_ref[q, :qlen] * factors[q : q + 1, :] - sums_ref[q, qlen:]
 
 
 def body(query_tokens, passage_tokens, passage_lengths, cand_shard, cand_local, teacher_scores):
@@ -353,7 +358,7 @@
         [VMEM, VMEM, VMEM],
         int(1e9),
     )(parts, own, sums)
-    sent = lax.all_to_all(grads, "passage", 0, 0, tiled=True)
+    sent = lax.all_to_all(grads, "passage", 0, 0, tiled=True, axis_index_groups=[turns(shards)])
     left = [list(members) for members in zip(*told)]
     loss = jnp.sum(lax.all_gather(loss, "query", axis=0, tiled=True, axis_index_groups=left), axis=0, keepdims=True)
     query_grads = jnp.sum(sent, axis=0, keepdims=True)

time: 77.2 us -> 75.3 us (0.975)
  Pallas kernels: 17.6 us -> 12.5 us
  starting transfers between devices: 24.7 us -> 26.1 us
  waiting for transfers between devices: 13.9 us -> 14.9 us
    pallas_call x1, Pallas kernels: 8.19 us -> 5.53 us  [body(): call(score, (pltpu.HBM((units, SLOTS * qlen, plen), bf16), pltpu.HBM((uni...]
    all_to_all x1, starting transfers between devices: 9.1 us -> 11.7 us  [body(): lax.all_to_all(local.reshape(TOLD * shards, 1, LANES), ('query', 'passage...]
    pallas_call x1, Pallas kernels: 6.8 us -> 4.32 us  [body(): call(terms_of, (held((group + 1, 2 * qlen, dim), f32),), [SMEM, HBM, VMEM...]
    all_to_all x1, waiting for transfers between devices: 3.84 us -> 6.32 us  [body(): lax.all_to_all(local.reshape(TOLD * shards, 1, LANES), ('query', 'passage...]
    all_to_all x1, waiting for transfers between devices: 2.76 us -> 1.35 us  [body(): lax.all_to_all(grads, 'passage', 0, 0, tiled=True, axis_index_groups=[tur...]
    all_to_all x1, starting transfers between devices: 5.08 us -> 3.89 us  [body(): lax.all_to_all(grads, 'passage', 0, 0, tiled=True, axis_index_groups=[tur...]
  transfers between devices with their start and end apart: 3 -> 3, of which waited for: 3 -> 3; matrix products, arithmetic and copies ran while one was open for 1% -> 1% of each run, Pallas kernels for 11% -> 8%
where the time goes in v7:
time: 75.3 us; the launch traced here: 74.2 us
  starting transfers between devices  26.1 us (35%)
  waiting for transfers between devices  14.9 us (20%)
  blocking collectives  14.3 us (19%)
  Pallas kernels  12.5 us (17%)
  local copies, waits for them, and re-layouts  3.8 us (5%)
  between operations  1.87 us (2%)
    all_gather x1, blocking collectives, body(): lax.all_gather(loss, 'query', axis=0, tiled=True, axis_index_groups=left)  14.3 us
    all_to_all x1, starting transfers between devices, body(): lax.all_to_all(local.reshape(TOLD * shards, 1, LANES), ('query', 'passage...  11.7 us
    all_to_all x1, starting transfers between devices, body(): lax.all_to_all(jnp.broadcast_to(query_tokens, (shards, qlen, dim)), 'pass...  10.5 us
    all_to_all x1, waiting for transfers between devices, body(): lax.all_to_all(jnp.broadcast_to(query_tokens, (shards, qlen, dim)), 'pass...  7.27 us
    all_to_all x1, waiting for transfers between devices, body(): lax.all_to_all(local.reshape(TOLD * shards, 1, LANES), ('query', 'passage...  6.32 us
    pallas_call x1, Pallas kernels, body(): call(score, (pltpu.HBM((units, SLOTS * qlen, plen), bf16), pltpu.HBM((uni...  5.53 us
    pallas_call x1, Pallas kernels, body(): call(terms_of, (held((group + 1, 2 * qlen, dim), f32),), [SMEM, HBM, VMEM...  4.32 us
    all_to_all x1, starting transfers between devices, body(): lax.all_to_all(grads, 'passage', 0, 0, tiled=True, axis_index_groups=[tur...  3.89 us
  transfers between devices with their start and end apart: 3, of which 3 were waited for; matrix products, arithmetic and copies ran while one was open for 1% of the time, Pallas kernels for 8%

profile of v7, /device:TPU:1, one launch (start us, length us, event | category | flops | bytes accessed | tf_op | source)
XLA Modules:
  0.0 74.2 jit_solution(2732256137649059093)
XLA Ops:
  0.6 0.0 copy-start
  0.6 1.4 %broadcast_in_dim.14 = bf16[32,32,128]{2,1,0:T(8,128)(2,1)} broadcast(bf16[32,128]{1,0:T(8,128)(2,1)} %bitcast.22), dimensions={1,2} | broadcast | bytes 270336 | tf_op jit(solution)/shard_map/broadcast_in_dim | solution.py:300
  2.1 10.5 %all-to-all-start = ((bf16[32,32,128]{2,1,0:T(8,128)(2,1)}), bf16[32,32,128]{2,1,0:T(8,128)(2,1)S(1)}, u32[]{:S(2)}, u32[]{:S(2)}) async-start(bf16[32,32,128]{2,1,0:T(8,128)(2,1)} %broadcast_in_dim.14), calls=%async_computation | async-start | bytes 524288 | tf_op jit(solution)/shard_map/all_to_all | solution.py:300
  12.6 0.8 %copy.11 = s32[32,256,1]{1,0,2:T(8,128)S(1)} copy(s32[32,256,1]{1,2,0:T(1,128)} %param.9) | data formatting | bytes 65536
  13.4 0.0 copy-done
  13.4 0.1 dynamic-slice_bitcast_fusion.lengths_ref
  13.4 0.0 copy-start.2
  13.4 0.8 %copy-done.2 = s32[32,256]{1,0:T(8,128)S(1)} copy-done((s32[32,256]{1,0:T(8,128)S(1)}, s32[32,256]{1,0:T(8,128)}, u32[]{:S(2)}) %copy-start.2) | copy-done | bytes 32792
  14.2 0.0 copy-start.3
  14.2 0.8 %copy-done.3 = f32[32,256]{1,0:T(8,128)S(1)} copy-done((f32[32,256]{1,0:T(8,128)S(1)}, f32[32,256]{1,0:T(8,128)}, u32[]{:S(2)}) %copy-start.3) | copy-done | bytes 32792
  15.0 0.0 copy-start.1
  15.0 1.6 %shard_map.77 = (s32[16,128]{1,0:T(8,128)S(1)}, f32[176,128]{1,0:T(8,128)S(1)}, f32[176,128]{1,0:T(8,128)S(1)}, f32[176,128]{1,0:T(8,128)S(1)}, f32[176,128]{1,0:T(8,128)S(1)}, /*index=5*/f32[1,128]{1,0:T(1,128)S(1)}) custom-call(s32[32,256]{1,0:T(8,128)S(1)} %bitcast.17, s32[32,256]{1,0:T(8,128)S(1)} %copy-done.2, f32[32,256]{1,0:T(8,128)S(1)} %copy-done.3, ...), custom_call_target="tpu_custom_call" | custom-call | flops 2000000000 | bytes 20000000 | tf_op jit(solution)/shard_map/pallas_call | solution.py:302
  16.5 7.3 %all-to-all-done.query_ref = bf16[32,32,128]{2,1,0:T(8,128)(2,1)S(1)} async-done(((bf16[32,32,128]{2,1,0:T(8,128)(2,1)}), bf16[32,32,128]{2,1,0:T(8,128)(2,1)S(1)}, u32[]{:S(2)}, u32[]{:S(2)}) %all-to-all-start) | async-done | bytes 262176 | tf_op jit(solution)/shard_map/all_to_all | solution.py:300
  23.8 0.0 copy-done.1
  23.8 5.5 %shard_map.78 = (bf16[176,128,128]{2,1,0:T(8,128)(2,1)}, f32[176,128]{1,0:T(8,128)}, f32[128,128]{1,0:T(8,128)}, f32[8,128]{1,0:T(8,128)S(1)}) custom-call(s32[2048]{0:T(1024)S(1)} %bitcast.19, bf16[32,32,128]{2,1,0:T(8,128)(2,1)S(1)} %all-to-all-done.query_ref, bf16[64,128,128]{2,1,0:T(8,128)(2,1)S(1)} %copy-done.1, ...), custom_call_target="tpu_custom_call" | custom-call | flops 4000000000 | bytes 40000000 | tf_op jit(solution)/shard_map/pallas_call | solution.py:315
  29.3 11.7 %all-to-all-start.1 = ((f32[128,1,128]{2,1,0:T(1,128)}), f32[128,1,128]{2,1,0:T(1,128)S(1)}, u32[]{:S(2)}, u32[]{:S(2)}) async-start(f32[128,1,128]{2,1,0:T(1,128)} %bitcast.4), calls=%async_computation.1 | async-start | bytes 131072 | tf_op jit(solution)/shard_map/all_to_all | solution.py:338
  41.0 4.3 %shard_map.79.sums_ref = f32[33,64,128]{2,1,0:T(8,128)S(1)} custom-call(s32[2048]{0:T(1024)S(1)} %bitcast.20, bf16[176,128,128]{2,1,0:T(8,128)(2,1)} %get-tuple-element.22.weight_ref, bf16[64,128,128]{2,1,0:T(8,128)(2,1)S(1)} %copy-done.1, f32[176,128]{1,0:T(8,128)} %get-tuple-element.23.factor_ref), custom_call_target="tpu_custom_call" | custom-call | flops 4000000000 | bytes 40000000 | tf_op jit(solution)/shard_map/pallas_call | solution.py:341
  45.4 6.3 %all-to-all-done.1 = f32[128,1,128]{2,1,0:T(1,128)S(1)} async-done(((f32[128,1,128]{2,1,0:T(1,128)}), f32[128,1,128]{2,1,0:T(1,128)S(1)}, u32[]{:S(2)}, u32[]{:S(2)}) %all-to-all-start.1) | async-done | bytes 65568 | tf_op jit(solution)/shard_map/all_to_all | solution.py:338
  51.7 1.1 %shard_map.80 = (f32[32,32,128]{2,1,0:T(8,128)}, f32[1,128]{1,0:T(1,128)S(1)}) custom-call(f32[128,128]{1,0:T(8,128)S(1)} %bitcast.16, f32[8,128]{1,0:T(8,128)S(1)} %get-tuple-element.21.own_ref, f32[33,64,128]{2,1,0:T(8,128)S(1)} %shard_map.79.sums_ref), custom_call_target="tpu_custom_call" | custom-call | flops 1000000000 | bytes 10000000 | tf_op jit(solution)/shard_map/pallas_call | solution.py:355
  52.8 3.9 %all-to-all-start.2 = ((f32[32,32,128]{2,1,0:T(8,128)}), f32[32,32,128]{2,1,0:T(8,128)S(1)}, u32[]{:S(2)}, u32[]{:S(2)}) async-start(f32[32,32,128]{2,1,0:T(8,128)} %get-tuple-element.25), calls=%async_computation.2 | async-start | bytes 1048576 | tf_op jit(solution)/shard_map/all_to_all | solution.py:361
  56.7 14.3 %all-gather = f32[4,1,128]{2,1,0:T(1,128)S(1)} all-gather(f32[1,1,128]{2,1,0:T(1,128)S(1)} %bitcast.18), channel_id=1, replica_groups={{0,128,256,384},{32,160,288,416},{64,192,320,448},{96,224,352,480},{1,1..., dimensions={0}, use_global_device_ids=true | all-gather | bytes 2560 | tf_op jit(solution)/shard_map/all_gather | solution.py:363
  71.1 1.4 %all-to-all-done.2 = f32[32,32,128]{2,1,0:T(8,128)S(1)} async-done(((f32[32,32,128]{2,1,0:T(8,128)}), f32[32,32,128]{2,1,0:T(8,128)S(1)}, u32[]{:S(2)}, u32[]{:S(2)}) %all-to-all-start.2) | async-done | bytes 524320 | tf_op jit(solution)/shard_map/all_to_all | solution.py:361
  72.4 0.6 reduce_sum.19
  (1 shorter events, 0.0 us)
Async XLA Ops:
  0.6 12.7 %copy-start = (s32[2048]{0:T(1024)S(1)}, s32[2048]{0:T(1024)}, u32[]{:S(2)}) copy-start(s32[2048]{0:T(1024)} %param.8) | copy-start | bytes 24580
  2.1 21.7 %all-to-all-start = ((bf16[32,32,128]{2,1,0:T(8,128)(2,1)}), bf16[32,32,128]{2,1,0:T(8,128)(2,1)S(1)}, u32[]{:S(2)}, u32[]{:S(2)}) async-start(bf16[32,32,128]{2,1,0:T(8,128)(2,1)} %broadcast_in_dim.14), calls=%async_computation | async-start | bytes 524288 | tf_op jit(solution)/shard_map/all_to_all | solution.py:300
  13.4 0.8 %copy-start.2 = (s32[32,256]{1,0:T(8,128)S(1)}, s32[32,256]{1,0:T(8,128)}, u32[]{:S(2)}) copy-start(s32[32,256]{1,0:T(8,128)} %local_ref.1) | copy-start | bytes 98308
  14.2 0.8 %copy-start.3 = (f32[32,256]{1,0:T(8,128)S(1)}, f32[32,256]{1,0:T(8,128)}, u32[]{:S(2)}) copy-start(f32[32,256]{1,0:T(8,128)} %teacher_ref.1) | copy-start | bytes 98308
  15.0 8.8 %copy-start.1 = (bf16[64,128,128]{2,1,0:T(8,128)(2,1)S(1)}, bf16[64,128,128]{2,1,0:T(8,128)(2,1)}, u32[]{:S(2)}) copy-start(bf16[64,128,128]{2,1,0:T(8,128)(2,1)} %passage_ref.3) | copy-start | bytes 6291460
  29.3 22.4 %all-to-all-start.1 = ((f32[128,1,128]{2,1,0:T(1,128)}), f32[128,1,128]{2,1,0:T(1,128)S(1)}, u32[]{:S(2)}, u32[]{:S(2)}) async-start(f32[128,1,128]{2,1,0:T(1,128)} %bitcast.4), calls=%async_computation.1 | async-start | bytes 131072 | tf_op jit(solution)/shard_map/all_to_all | solution.py:338
  52.8 19.7 %all-to-all-start.2 = ((f32[32,32,128]{2,1,0:T(8,128)}), f32[32,32,128]{2,1,0:T(8,128)S(1)}, u32[]{:S(2)}, u32[]{:S(2)}) async-start(f32[32,32,128]{2,1,0:T(8,128)} %get-tuple-element.25), calls=%async_computation.2 | async-start | bytes 1048576 | tf_op jit(solution)/shard_map/all_to_all | solution.py:361

commit v8 on v6

--- a/solution.py
+++ b/solution.py
@@ -176,7 +176,12 @@
     lax.fori_loop(0, rounds + 1, some, 0)
     same = iota((columns, LANES), 0) // qlen == iota((columns, LANES), 1)
     rows = row_ref[pl.ds(AHEAD, units), :]
-    summed = jnp.dot(rows, jnp.where(same, 0.5, 0.0), preferred_element_type=f32, precision=lax.Precision.HIGHEST)
+    halves = jnp.where(same, 0.5, 0.0).astype(bf16)
+    summed = jnp.zeros((units, LANES), f32)
+    for _ in range(3):
+        part = rows.astype(bf16)
+        summed += jnp.dot(part, halves, preferred_element_type=f32)
+        rows -= part.astype(f32)
     slot, count, mass = slot_ref[...], count_ref[...], mass_ref[...]
     scores = jnp.zeros((units, LANES), f32)
     for k in range(SLOTS):

time: 77.2 us -> 76.3 us (0.988)
  Pallas kernels: 17.6 us -> 12.5 us
  waiting for transfers between devices: 13.9 us -> 16.1 us
  starting transfers between devices: 24.7 us -> 26.4 us
    pallas_call x1, Pallas kernels: 8.19 us -> 5.51 us  [body(): call(score, (pltpu.HBM((units, SLOTS * qlen, plen), bf16), pltpu.HBM((uni...]
    pallas_call x1, Pallas kernels: 6.8 us -> 4.34 us  [body(): call(terms_of, (held((group + 1, 2 * qlen, dim), f32),), [SMEM, HBM, VMEM...]
    all_to_all x1, waiting for transfers between devices: 3.84 us -> 6.31 us  [body(): lax.all_to_all(local.reshape(TOLD * shards, 1, LANES), ('query', 'passage...]
    all_to_all x1, starting transfers between devices: 9.1 us -> 11.6 us  [body(): lax.all_to_all(local.reshape(TOLD * shards, 1, LANES), ('query', 'passage...]
  transfers between devices with their start and end apart: 3 -> 3, of which waited for: 3 -> 3; matrix products, arithmetic and copies ran while one was open for 1% -> 1% of each run, Pallas kernels for 11% -> 8%
where the time goes in v8:
time: 76.3 us; the launch traced here: 75.3 us
  starting transfers between devices  26.4 us (35%)
  waiting for transfers between devices  16.1 us (21%)
  blocking collectives  14 us (18%)
  Pallas kernels  12.5 us (16%)
  local copies, waits for them, and re-layouts  3.8 us (5%)
  between operations  1.87 us (2%)
    all_gather x1, blocking collectives, body(): lax.all_gather(loss, 'query', axis=0, tiled=True, axis_index_groups=left)  14 us
    all_to_all x1, starting transfers between devices, body(): lax.all_to_all(local.reshape(TOLD * shards, 1, LANES), ('query', 'passage...  11.6 us
    all_to_all x1, starting transfers between devices, body(): lax.all_to_all(jnp.broadcast_to(query_tokens, (shards, qlen, dim)), 'pass...  10.5 us
    all_to_all x1, waiting for transfers between devices, body(): lax.all_to_all(jnp.broadcast_to(query_tokens, (shards, qlen, dim)), 'pass...  7.27 us
    all_to_all x1, waiting for transfers between devices, body(): lax.all_to_all(local.reshape(TOLD * shards, 1, LANES), ('query', 'passage...  6.31 us
    pallas_call x1, Pallas kernels, body(): call(score, (pltpu.HBM((units, SLOTS * qlen, plen), bf16), pltpu.HBM((uni...  5.51 us
    pallas_call x1, Pallas kernels, body(): call(terms_of, (held((group + 1, 2 * qlen, dim), f32),), [SMEM, HBM, VMEM...  4.34 us
    all_to_all x1, starting transfers between devices, body(): sent = lax.all_to_all(grads, 'passage', 0, 0, tiled=True)  4.31 us
  transfers between devices with their start and end apart: 3, of which 3 were waited for; matrix products, arithmetic and copies ran while one was open for 1% of the time, Pallas kernels for 8%

profile of v8, /device:TPU:1, one launch (start us, length us, event | category | flops | bytes accessed | tf_op | source)
XLA Modules:
  0.0 75.3 jit_solution(15670104958971768797)
XLA Ops:
  0.6 0.0 copy-start
  0.6 1.4 %broadcast_in_dim.14 = bf16[32,32,128]{2,1,0:T(8,128)(2,1)} broadcast(bf16[32,128]{1,0:T(8,128)(2,1)} %bitcast.22), dimensions={1,2} | broadcast | bytes 270336 | tf_op jit(solution)/shard_map/broadcast_in_dim | solution.py:300
  2.1 10.5 %all-to-all-start = ((bf16[32,32,128]{2,1,0:T(8,128)(2,1)}), bf16[32,32,128]{2,1,0:T(8,128)(2,1)S(1)}, u32[]{:S(2)}, u32[]{:S(2)}) async-start(bf16[32,32,128]{2,1,0:T(8,128)(2,1)} %broadcast_in_dim.14), calls=%async_computation | async-start | bytes 524288 | tf_op jit(solution)/shard_map/all_to_all | solution.py:300
  12.6 0.8 %copy.11 = s32[32,256,1]{1,0,2:T(8,128)S(1)} copy(s32[32,256,1]{1,2,0:T(1,128)} %param.9) | data formatting | bytes 65536
  13.4 0.0 copy-done
  13.4 0.1 dynamic-slice_bitcast_fusion.lengths_ref
  13.4 0.0 copy-start.2
  13.4 0.8 %copy-done.2 = s32[32,256]{1,0:T(8,128)S(1)} copy-done((s32[32,256]{1,0:T(8,128)S(1)}, s32[32,256]{1,0:T(8,128)}, u32[]{:S(2)}) %copy-start.2) | copy-done | bytes 32792
  14.2 0.0 copy-start.3
  14.2 0.8 %copy-done.3 = f32[32,256]{1,0:T(8,128)S(1)} copy-done((f32[32,256]{1,0:T(8,128)S(1)}, f32[32,256]{1,0:T(8,128)}, u32[]{:S(2)}) %copy-start.3) | copy-done | bytes 32792
  15.0 0.0 copy-start.1
  15.0 1.6 %shard_map.77 = (s32[16,128]{1,0:T(8,128)S(1)}, f32[176,128]{1,0:T(8,128)S(1)}, f32[176,128]{1,0:T(8,128)S(1)}, f32[176,128]{1,0:T(8,128)S(1)}, f32[176,128]{1,0:T(8,128)S(1)}, /*index=5*/f32[1,128]{1,0:T(1,128)S(1)}) custom-call(s32[32,256]{1,0:T(8,128)S(1)} %bitcast.17, s32[32,256]{1,0:T(8,128)S(1)} %copy-done.2, f32[32,256]{1,0:T(8,128)S(1)} %copy-done.3, ...), custom_call_target="tpu_custom_call" | custom-call | flops 2000000000 | bytes 20000000 | tf_op jit(solution)/shard_map/pallas_call | solution.py:302
  16.5 7.3 %all-to-all-done.query_ref = bf16[32,32,128]{2,1,0:T(8,128)(2,1)S(1)} async-done(((bf16[32,32,128]{2,1,0:T(8,128)(2,1)}), bf16[32,32,128]{2,1,0:T(8,128)(2,1)S(1)}, u32[]{:S(2)}, u32[]{:S(2)}) %all-to-all-start) | async-done | bytes 262176 | tf_op jit(solution)/shard_map/all_to_all | solution.py:300
  23.8 0.0 copy-done.1
  23.8 5.5 %shard_map.78 = (bf16[176,128,128]{2,1,0:T(8,128)(2,1)}, f32[176,128]{1,0:T(8,128)}, f32[128,128]{1,0:T(8,128)}, f32[8,128]{1,0:T(8,128)S(1)}) custom-call(s32[2048]{0:T(1024)S(1)} %bitcast.19, bf16[32,32,128]{2,1,0:T(8,128)(2,1)S(1)} %all-to-all-done.query_ref, bf16[64,128,128]{2,1,0:T(8,128)(2,1)S(1)} %copy-done.1, ...), custom_call_target="tpu_custom_call" | custom-call | flops 4000000000 | bytes 40000000 | tf_op jit(solution)/shard_map/pallas_call | solution.py:315
  29.3 11.6 %all-to-all-start.1 = ((f32[128,1,128]{2,1,0:T(1,128)}), f32[128,1,128]{2,1,0:T(1,128)S(1)}, u32[]{:S(2)}, u32[]{:S(2)}) async-start(f32[128,1,128]{2,1,0:T(1,128)} %bitcast.4), calls=%async_computation.1 | async-start | bytes 131072 | tf_op jit(solution)/shard_map/all_to_all | solution.py:338
  40.9 4.3 %shard_map.79.sums_ref = f32[33,64,128]{2,1,0:T(8,128)S(1)} custom-call(s32[2048]{0:T(1024)S(1)} %bitcast.20, bf16[176,128,128]{2,1,0:T(8,128)(2,1)} %get-tuple-element.22.weight_ref, bf16[64,128,128]{2,1,0:T(8,128)(2,1)S(1)} %copy-done.1, f32[176,128]{1,0:T(8,128)} %get-tuple-element.23.factor_ref), custom_call_target="tpu_custom_call" | custom-call | flops 4000000000 | bytes 40000000 | tf_op jit(solution)/shard_map/pallas_call | solution.py:341
  45.2 6.3 %all-to-all-done.1 = f32[128,1,128]{2,1,0:T(1,128)S(1)} async-done(((f32[128,1,128]{2,1,0:T(1,128)}), f32[128,1,128]{2,1,0:T(1,128)S(1)}, u32[]{:S(2)}, u32[]{:S(2)}) %all-to-all-start.1) | async-done | bytes 65568 | tf_op jit(solution)/shard_map/all_to_all | solution.py:338
  51.5 1.1 %shard_map.80 = (f32[32,32,128]{2,1,0:T(8,128)}, f32[1,128]{1,0:T(1,128)S(1)}) custom-call(f32[128,128]{1,0:T(8,128)S(1)} %bitcast.16, f32[8,128]{1,0:T(8,128)S(1)} %get-tuple-element.21.own_ref, f32[33,64,128]{2,1,0:T(8,128)S(1)} %shard_map.79.sums_ref), custom_call_target="tpu_custom_call" | custom-call | flops 1000000000 | bytes 10000000 | tf_op jit(solution)/shard_map/pallas_call | solution.py:355
  52.6 4.3 %all-to-all-start.2 = ((f32[32,32,128]{2,1,0:T(8,128)}), f32[32,32,128]{2,1,0:T(8,128)S(1)}, u32[]{:S(2)}, u32[]{:S(2)}) async-start(f32[32,32,128]{2,1,0:T(8,128)} %get-tuple-element.25), calls=%async_computation.2 | async-start | bytes 1048576 | tf_op jit(solution)/shard_map/all_to_all | solution.py:361
  56.9 14.0 %all-gather = f32[4,1,128]{2,1,0:T(1,128)S(1)} all-gather(f32[1,1,128]{2,1,0:T(1,128)S(1)} %bitcast.18), channel_id=1, replica_groups={{0,128,256,384},{32,160,288,416},{64,192,320,448},{96,224,352,480},{1,1..., dimensions={0}, use_global_device_ids=true | all-gather | bytes 2560 | tf_op jit(solution)/shard_map/all_gather | solution.py:363
  71.0 2.5 %all-to-all-done.2 = f32[32,32,128]{2,1,0:T(8,128)S(1)} async-done(((f32[32,32,128]{2,1,0:T(8,128)}), f32[32,32,128]{2,1,0:T(8,128)S(1)}, u32[]{:S(2)}, u32[]{:S(2)}) %all-to-all-start.2) | async-done | bytes 524320 | tf_op jit(solution)/shard_map/all_to_all | solution.py:361
  73.5 0.6 reduce_sum.19
  (1 shorter events, 0.0 us)
Async XLA Ops:
  0.6 12.7 %copy-start = (s32[2048]{0:T(1024)S(1)}, s32[2048]{0:T(1024)}, u32[]{:S(2)}) copy-start(s32[2048]{0:T(1024)} %param.8) | copy-start | bytes 24580
  2.1 21.7 %all-to-all-start = ((bf16[32,32,128]{2,1,0:T(8,128)(2,1)}), bf16[32,32,128]{2,1,0:T(8,128)(2,1)S(1)}, u32[]{:S(2)}, u32[]{:S(2)}) async-start(bf16[32,32,128]{2,1,0:T(8,128)(2,1)} %broadcast_in_dim.14), calls=%async_computation | async-start | bytes 524288 | tf_op jit(solution)/shard_map/all_to_all | solution.py:300
  13.4 0.8 %copy-start.2 = (s32[32,256]{1,0:T(8,128)S(1)}, s32[32,256]{1,0:T(8,128)}, u32[]{:S(2)}) copy-start(s32[32,256]{1,0:T(8,128)} %local_ref.1) | copy-start | bytes 98308
  14.2 0.8 %copy-start.3 = (f32[32,256]{1,0:T(8,128)S(1)}, f32[32,256]{1,0:T(8,128)}, u32[]{:S(2)}) copy-start(f32[32,256]{1,0:T(8,128)} %teacher_ref.1) | copy-start | bytes 98308
  15.0 8.8 %copy-start.1 = (bf16[64,128,128]{2,1,0:T(8,128)(2,1)S(1)}, bf16[64,128,128]{2,1,0:T(8,128)(2,1)}, u32[]{:S(2)}) copy-start(bf16[64,128,128]{2,1,0:T(8,128)(2,1)} %passage_ref.3) | copy-start | bytes 6291460
  29.3 22.2 %all-to-all-start.1 = ((f32[128,1,128]{2,1,0:T(1,128)}), f32[128,1,128]{2,1,0:T(1,128)S(1)}, u32[]{:S(2)}, u32[]{:S(2)}) async-start(f32[128,1,128]{2,1,0:T(1,128)} %bitcast.4), calls=%async_computation.1 | async-start | bytes 131072 | tf_op jit(solution)/shard_map/all_to_all | solution.py:338
  52.6 20.9 %all-to-all-start.2 = ((f32[32,32,128]{2,1,0:T(8,128)}), f32[32,32,128]{2,1,0:T(8,128)S(1)}, u32[]{:S(2)}, u32[]{:S(2)}) async-start(f32[32,32,128]{2,1,0:T(8,128)} %get-tuple-element.25), calls=%async_computation.2 | async-start | bytes 1048576 | tf_op jit(solution)/shard_map/all_to_all | solution.py:361

commit v9 on v7

--- a/solution.py
+++ b/solution.py
@@ -181,7 +181,12 @@
     lax.fori_loop(0, rounds + 1, some, 0)
     same = iota((columns, LANES), 0) // qlen == iota((columns, LANES), 1)
     rows = row_ref[pl.ds(AHEAD, units), :]
-    summed = jnp.dot(rows, jnp.where(same, 0.5, 0.0), preferred_element_type=f32, precision=lax.Precision.HIGHEST)
+    halves = jnp.where(same, 0.5, 0.0).astype(bf16)
+    summed = jnp.zeros((units, LANES), f32)
+    for _ in range(3):
+        part = rows.astype(bf16)
+        summed += jnp.dot(part, halves, preferred_element_type=f32)
+        rows -= part.astype(f32)
     slot, count, mass = slot_ref[...], count_ref[...], mass_ref[...]
     scores = jnp.zeros((units, LANES), f32)
     for k in range(SLOTS):

time: 75.3 us -> 76 us (level); the launches traced: 74.2 us -> 75.9 us
  Pallas kernels: 12.5 us -> 14.5 us
    all_to_all x1, waiting for transfers between devices: 1.35 us -> 2.49 us  [body(): lax.all_to_all(grads, 'passage', 0, 0, tiled=True, axis_index_groups=[tur...]
    pallas_call x1, Pallas kernels: 5.53 us -> 6.57 us  [body(): call(score, (pltpu.HBM((units, SLOTS * qlen, plen), bf16), pltpu.HBM((uni...]
    all_to_all x1, waiting for transfers between devices: 6.32 us -> 5.35 us  [body(): lax.all_to_all(local.reshape(TOLD * shards, 1, LANES), ('query', 'passage...]
    pallas_call x1, Pallas kernels: 4.32 us -> 5.29 us  [body(): call(terms_of, (held((group + 1, 2 * qlen, dim), f32),), [SMEM, HBM, VMEM...]
    all_to_all x1, starting transfers between devices: 11.7 us -> 10.8 us  [body(): lax.all_to_all(local.reshape(TOLD * shards, 1, LANES), ('query', 'passage...]
  transfers between devices with their start and end apart: 3 -> 3, of which waited for: 3 -> 3; matrix products, arithmetic and copies ran while one was open for 1% -> 1% of each run, Pallas kernels for 8% -> 9%
where the time goes in v9:
time: 76 us; the launch traced here: 75.9 us
  starting transfers between devices  25.7 us (34%)
  waiting for transfers between devices  15.1 us (20%)
  Pallas kernels  14.5 us (19%)
  blocking collectives  14.2 us (19%)
  local copies, waits for them, and re-layouts  3.8 us (5%)
  between operations  1.87 us (2%)
    all_gather x1, blocking collectives, body(): lax.all_gather(loss, 'query', axis=0, tiled=True, axis_index_groups=left)  14.2 us
    all_to_all x1, starting transfers between devices, body(): lax.all_to_all(local.reshape(TOLD * shards, 1, LANES), ('query', 'passage...  10.8 us
    all_to_all x1, starting transfers between devices, body(): lax.all_to_all(jnp.broadcast_to(query_tokens, (shards, qlen, dim)), 'pass...  10.5 us
    all_to_all x1, waiting for transfers between devices, body(): lax.all_to_all(jnp.broadcast_to(query_tokens, (shards, qlen, dim)), 'pass...  7.27 us
    pallas_call x1, Pallas kernels, body(): call(score, (pltpu.HBM((units, SLOTS * qlen, plen), bf16), pltpu.HBM((uni...  6.57 us
    all_to_all x1, waiting for transfers between devices, body(): lax.all_to_all(local.reshape(TOLD * shards, 1, LANES), ('query', 'passage...  5.35 us
    pallas_call x1, Pallas kernels, body(): call(terms_of, (held((group + 1, 2 * qlen, dim), f32),), [SMEM, HBM, VMEM...  5.29 us
    all_to_all x1, starting transfers between devices, body(): lax.all_to_all(grads, 'passage', 0, 0, tiled=True, axis_index_groups=[tur...  4.37 us
  transfers between devices with their start and end apart: 3, of which 3 were waited for; matrix products, arithmetic and copies ran while one was open for 1% of the time, Pallas kernels for 9%

profile of v9, /device:TPU:1, one launch (start us, length us, event | category | flops | bytes accessed | tf_op | source)
XLA Modules:
  0.0 75.9 jit_solution(12032175796166405576)
XLA Ops:
  0.6 0.0 copy-start
  0.6 1.4 %broadcast_in_dim.14 = bf16[32,32,128]{2,1,0:T(8,128)(2,1)} broadcast(bf16[32,128]{1,0:T(8,128)(2,1)} %bitcast.22), dimensions={1,2} | broadcast | bytes 270336 | tf_op jit(solution)/shard_map/broadcast_in_dim | solution.py:305
  2.1 10.5 %all-to-all-start = ((bf16[32,32,128]{2,1,0:T(8,128)(2,1)}), bf16[32,32,128]{2,1,0:T(8,128)(2,1)S(1)}, u32[]{:S(2)}, u32[]{:S(2)}) async-start(bf16[32,32,128]{2,1,0:T(8,128)(2,1)} %broadcast_in_dim.14), calls=%async_computation | async-start | bytes 524288 | tf_op jit(solution)/shard_map/all_to_all | solution.py:305
  12.6 0.8 %copy.11 = s32[32,256,1]{1,0,2:T(8,128)S(1)} copy(s32[32,256,1]{1,2,0:T(1,128)} %param.9) | data formatting | bytes 65536
  13.4 0.0 copy-done
  13.4 0.1 dynamic-slice_bitcast_fusion.lengths_ref
  13.4 0.0 copy-start.2
  13.4 0.8 copy-done.2
  14.2 0.0 copy-start.3
  14.2 0.8 copy-done.3
  15.0 0.0 copy-start.1
  15.0 1.6 %shard_map.77 = (s32[16,128]{1,0:T(8,128)S(1)}, f32[176,128]{1,0:T(8,128)S(1)}, f32[176,128]{1,0:T(8,128)S(1)}, f32[176,128]{1,0:T(8,128)S(1)}, f32[176,128]{1,0:T(8,128)S(1)}, /*index=5*/f32[1,128]{1,0:T(1,128)S(1)}) custom-call(s32[32,256]{1,0:T(8,128)S(1)} %bitcast.17, s32[32,256]{1,0:T(8,128)S(1)} %copy-done.2, f32[32,256]{1,0:T(8,128)S(1)} %copy-done.3, ...), custom_call_target="tpu_custom_call" | custom-call | flops 2000000000 | bytes 20000000 | tf_op jit(solution)/shard_map/pallas_call | solution.py:307
  16.5 7.3 %all-to-all-done.query_ref = bf16[32,32,128]{2,1,0:T(8,128)(2,1)S(1)} async-done(((bf16[32,32,128]{2,1,0:T(8,128)(2,1)}), bf16[32,32,128]{2,1,0:T(8,128)(2,1)S(1)}, u32[]{:S(2)}, u32[]{:S(2)}) %all-to-all-start) | async-done | bytes 262176 | tf_op jit(solution)/shard_map/all_to_all | solution.py:305
  23.8 0.0 copy-done.1
  23.8 6.6 %shard_map.78 = (bf16[176,128,128]{2,1,0:T(8,128)(2,1)}, f32[176,128]{1,0:T(8,128)}, f32[128,128]{1,0:T(8,128)}, f32[8,128]{1,0:T(8,128)S(1)}) custom-call(s32[2048]{0:T(1024)S(1)} %bitcast.19, bf16[32,32,128]{2,1,0:T(8,128)(2,1)S(1)} %all-to-all-done.query_ref, bf16[64,128,128]{2,1,0:T(8,128)(2,1)S(1)} %copy-done.1, ...), custom_call_target="tpu_custom_call" | custom-call | flops 4000000000 | bytes 40000000 | tf_op jit(solution)/shard_map/pallas_call | solution.py:320
  30.4 10.8 %all-to-all-start.1 = ((f32[128,1,128]{2,1,0:T(1,128)}), f32[128,1,128]{2,1,0:T(1,128)S(1)}, u32[]{:S(2)}, u32[]{:S(2)}) async-start(f32[128,1,128]{2,1,0:T(1,128)} %bitcast.4), calls=%async_computation.1 | async-start | bytes 131072 | tf_op jit(solution)/shard_map/all_to_all | solution.py:343
  41.2 5.3 %shard_map.79.sums_ref = f32[33,64,128]{2,1,0:T(8,128)S(1)} custom-call(s32[2048]{0:T(1024)S(1)} %bitcast.20, bf16[176,128,128]{2,1,0:T(8,128)(2,1)} %get-tuple-element.22.weight_ref, bf16[64,128,128]{2,1,0:T(8,128)(2,1)S(1)} %copy-done.1, f32[176,128]{1,0:T(8,128)} %get-tuple-element.23.factor_ref), custom_call_target="tpu_custom_call" | custom-call | flops 4000000000 | bytes 40000000 | tf_op jit(solution)/shard_map/pallas_call | solution.py:346
  46.5 5.4 %all-to-all-done.1 = f32[128,1,128]{2,1,0:T(1,128)S(1)} async-done(((f32[128,1,128]{2,1,0:T(1,128)}), f32[128,1,128]{2,1,0:T(1,128)S(1)}, u32[]{:S(2)}, u32[]{:S(2)}) %all-to-all-start.1) | async-done | bytes 65568 | tf_op jit(solution)/shard_map/all_to_all | solution.py:343
  51.8 1.1 %shard_map.80 = (f32[32,32,128]{2,1,0:T(8,128)}, f32[1,128]{1,0:T(1,128)S(1)}) custom-call(f32[128,128]{1,0:T(8,128)S(1)} %bitcast.16, f32[8,128]{1,0:T(8,128)S(1)} %get-tuple-element.21.own_ref, f32[33,64,128]{2,1,0:T(8,128)S(1)} %shard_map.79.sums_ref), custom_call_target="tpu_custom_call" | custom-call | flops 1000000000 | bytes 10000000 | tf_op jit(solution)/shard_map/pallas_call | solution.py:360
  52.9 4.4 %all-to-all-start.2 = ((f32[32,32,128]{2,1,0:T(8,128)}), f32[32,32,128]{2,1,0:T(8,128)S(1)}, u32[]{:S(2)}, u32[]{:S(2)}) async-start(f32[32,32,128]{2,1,0:T(8,128)} %get-tuple-element.25), calls=%async_computation.2 | async-start | bytes 1048576 | tf_op jit(solution)/shard_map/all_to_all | solution.py:366
  57.3 14.2 %all-gather = f32[4,1,128]{2,1,0:T(1,128)S(1)} all-gather(f32[1,1,128]{2,1,0:T(1,128)S(1)} %bitcast.18), channel_id=1, replica_groups={{0,128,256,384},{32,160,288,416},{64,192,320,448},{96,224,352,480},{1,1..., dimensions={0}, use_global_device_ids=true | all-gather | bytes 2560 | tf_op jit(solution)/shard_map/all_gather | solution.py:368
  71.6 2.5 %all-to-all-done.2 = f32[32,32,128]{2,1,0:T(8,128)S(1)} async-done(((f32[32,32,128]{2,1,0:T(8,128)}), f32[32,32,128]{2,1,0:T(8,128)S(1)}, u32[]{:S(2)}, u32[]{:S(2)}) %all-to-all-start.2) | async-done | bytes 524320 | tf_op jit(solution)/shard_map/all_to_all | solution.py:366
  74.1 0.6 reduce_sum.19
  (1 shorter events, 0.0 us)
Async XLA Ops:
  0.6 12.7 %copy-start = (s32[2048]{0:T(1024)S(1)}, s32[2048]{0:T(1024)}, u32[]{:S(2)}) copy-start(s32[2048]{0:T(1024)} %param.8) | copy-start | bytes 24580
  2.1 21.7 %all-to-all-start = ((bf16[32,32,128]{2,1,0:T(8,128)(2,1)}), bf16[32,32,128]{2,1,0:T(8,128)(2,1)S(1)}, u32[]{:S(2)}, u32[]{:S(2)}) async-start(bf16[32,32,128]{2,1,0:T(8,128)(2,1)} %broadcast_in_dim.14), calls=%async_computation | async-start | bytes 524288 | tf_op jit(solution)/shard_map/all_to_all | solution.py:305
  13.4 0.8 copy-start.2
  14.2 0.8 copy-start.3
  15.0 8.8 %copy-start.1 = (bf16[64,128,128]{2,1,0:T(8,128)(2,1)S(1)}, bf16[64,128,128]{2,1,0:T(8,128)(2,1)}, u32[]{:S(2)}) copy-start(bf16[64,128,128]{2,1,0:T(8,128)(2,1)} %passage_ref.3) | copy-start | bytes 6291460
  30.4 21.5 %all-to-all-start.1 = ((f32[128,1,128]{2,1,0:T(1,128)}), f32[128,1,128]{2,1,0:T(1,128)S(1)}, u32[]{:S(2)}, u32[]{:S(2)}) async-start(f32[128,1,128]{2,1,0:T(1,128)} %bitcast.4), calls=%async_computation.1 | async-start | bytes 131072 | tf_op jit(solution)/shard_map/all_to_all | solution.py:343
  52.9 21.2 %all-to-all-start.2 = ((f32[32,32,128]{2,1,0:T(8,128)}), f32[32,32,128]{2,1,0:T(8,128)S(1)}, u32[]{:S(2)}, u32[]{:S(2)}) async-start(f32[32,32,128]{2,1,0:T(8,128)} %get-tuple-element.25), calls=%async_computation.2 | async-start | bytes 1048576 | tf_op jit(solution)/shard_map/all_to_all | solution.py:366
